TPU v7x, 32 devices: a whole 2x2x4 slice. The times are simulated.
32 devices in a mesh: rep: 2 (over y), inst: 4 (over z), tp: 4 (over x, core).
Axes of the slice: x: 2, y: 2, z: 4, core: 2. Of those that a mesh axis runs over, the one named last changes fastest.
Arguments:
- dest_slot: int32 [112], P('rep'), parts along dimension 0, may hold values from 0 to 55, as said below
- finished: int32 [112], P(('rep', 'inst')), parts along dimension 0, may hold values from 0 to 1, as said below
- lengths: int32 [112], P(('rep', 'inst')), parts along dimension 0, may hold values from 1 to 128
- cache_keys: bfloat16 [112, 256, 1024], P(('rep', 'inst'), None, 'tp'), parts along dimension 0, may hold values from -6 to 6
- cache_values: bfloat16 [112, 256, 1024], P(('rep', 'inst'), None, 'tp'), parts along dimension 0, may hold values from -6 to 6
- responses: bfloat16 [112, 128, 3072], P(('rep', 'inst'), None, 'tp'), parts along dimension 0, may hold values from -6 to 6
- dec_queries: bfloat16 [112, 2, 4096], P(('rep', 'inst'), None, 'tp'), parts along dimension 0, may hold values from -6 to 6
- new_keys: bfloat16 [112, 2, 1024], P(('rep', 'inst'), None, 'tp'), parts along dimension 0, may hold values from -6 to 6
- new_values: bfloat16 [112, 2, 1024], P(('rep', 'inst'), None, 'tp'), parts along dimension 0, may hold values from -6 to 6
- norm_gain: float32 [3072], replicated, may hold values from 0.5 to 2
- w_query: bfloat16 [3072, 4096], P(None, 'tp'), may hold values from -0.108253175 to 0.108253175
- w_key: bfloat16 [3072, 1024], P(None, 'tp'), may hold values from -0.108253175 to 0.108253175
- w_value: bfloat16 [3072, 1024], P(None, 'tp'), may hold values from -0.109375 to 0.109375
- w_out: bfloat16 [4096, 3072], P('tp'), may hold values from -0.09375 to 0.09375
Outputs:
- decode_out: bfloat16 [112, 2, 4096], P(('rep', 'inst'), None, 'tp'), parts along dimension 0
- prefill_out: bfloat16 [112, 128, 3072], P(('rep', 'inst'), None, 'tp'), parts along dimension 0
There are 2 independent parts, one for each index of `rep`. A program takes and returns all parts, laid end to end along the dimension named above; an argument that names none is the same for every part. Nothing has to cross between parts.
Inputs may be any that keep to these rules, and one draw needn't show every extreme that they name: `dest_slot`: A permutation of the slots; slot s lies on instance s // 14. Row j of instance i goes to instance (i + a shift that depends on j only) mod 4; every shift used is used by exactly 7 values of j, so each instance sends its rows in groups of 7 to 2 distinct instances, and each instance receives 14 rows. The shifts used are 1 and 2. The rows that one instance receives are all unfinished or all finished; exactly 1 instance receives unfinished rows.
All inputs are finite; a program needn't handle non-finite values.
Results may differ from a plain program's by a relative error of at most 0.011.
Values may be sent and summed in bfloat16 or wider, within the bound.
No kernel may reach another device: no remote copies, remote signals or barrier semaphores. Data moves between devices by JAX's collectives and lax.ppermute only.
A program may use at most 128 MiB of HBM per device.

v0:
```python
import math

import jax
import jax.numpy as jnp
from jax import lax
from jax.experimental import pallas as pl
from jax.experimental.pallas import tpu as pltpu
from jax.sharding import PartitionSpec as P

QH = 32
KVH = 8
HD = 128
PROMPT = 128


BLOCK = 64
TILE = 512
COST = 3
NEAR_SHARES = (320, 384)
FAR_SHARES = (256, 256, 192)
NEG = -1e30
CAPACITY = 704


def layer_kernel(
    base,
    part_ref,
    start_ref,
    own_ref,
    across_ref,
    beside_ref,
    earlier_ref,
    gain_ref,
    wq_ref,
    wk_ref,
    wv_ref,
    w_out,
    send_ref,
    keep_ref,
    later_ref,
    states,
    inverse,
    qkv,
    attended,
):
    tokens, width = own_ref.shape
    features = states.shape[1]
    q_width = w_out.shape[0]
    kv_width = wk_ref.shape[1]
    group_size = QH // KVH
    part = part_ref[0]

    def columns_of(block):
        return pl.ds(pl.multiple_of(block * width, 128), width)

    states[:, columns_of(part)] = own_ref[...]
    states[:, columns_of(part ^ 2)] = across_ref[...]
    states[:, columns_of(part ^ 1)] = beside_ref[:, :width]
    states[:, columns_of(part ^ 3)] = beside_ref[:, width:]
    qkv[:PROMPT, q_width:] = earlier_ref[...]

    def norm_rows(b, carry):
        rows = pl.ds(pl.multiple_of(b * BLOCK, BLOCK), BLOCK)
        total = jnp.zeros((BLOCK, 128), jnp.float32)
        for c in range(0, features, 128):
            value = states[rows, c : c + 128].astype(jnp.float32) * gain_ref[:, c : c + 128]
            total = total + value * value
        mean = jnp.sum(total, axis=1, keepdims=True) * (1.0 / features)
        inverse[rows, :] = jnp.broadcast_to(lax.rsqrt(mean + 1e-06), (BLOCK, 128))
        return carry

    lax.fori_loop(0, tokens // BLOCK, norm_rows, 0)
    def project(t, carry):
        columns = pl.ds(pl.multiple_of(t * TILE, TILE), TILE)
        product = jnp.dot(states[...], wq_ref[:, columns], preferred_element_type=jnp.float32)
        scale = inverse[...] * (math.log2(math.e) / math.sqrt(HD))
        scale = jnp.concatenate([scale] * (TILE // 128), axis=1)
        qkv[PROMPT:, columns] = (product * scale).astype(jnp.bfloat16)
        return carry

    lax.fori_loop(0, q_width // TILE, project, 0)
    scale = jnp.concatenate([inverse[...]] * (kv_width // 128), axis=1)
    for first, w_ref in ((q_width, wk_ref), (q_width + kv_width, wv_ref)):
        product = jnp.dot(states[...], w_ref[...], preferred_element_type=jnp.float32)
        qkv[PROMPT:, first : first + kv_width] = (product * scale).astype(jnp.bfloat16)

    shape = (BLOCK, BLOCK + PROMPT)

    def attend(b, carry):
        row = pl.multiple_of(b * BLOCK, BLOCK)
        query_pos = base + row + lax.broadcasted_iota(jnp.int32, shape, 0)
        key_pos = base + row - PROMPT + lax.broadcasted_iota(jnp.int32, shape, 1)
        allowed = (key_pos >= start_ref[pl.ds(row, BLOCK), :]) & (key_pos <= query_pos)
        bias = jnp.where(allowed, 0.0, NEG)
        bias = jnp.concatenate([bias] * group_size, axis=0)
        query_rows = pl.ds(pl.multiple_of(row + PROMPT, BLOCK), BLOCK)
        key_rows = pl.ds(row, BLOCK + PROMPT)
        for head in range(kv_width // HD):
            columns = [(head * group_size + g) * HD for g in range(group_size)]
            queries = jnp.concatenate([qkv[query_rows, c : c + HD] for c in columns], axis=0)
            first = q_width + head * HD
            keys = qkv[key_rows, first : first + HD]
            values = qkv[key_rows, first + kv_width : first + kv_width + HD]
            scores = lax.dot_general(
                queries, keys, (((1,), (1,)), ((), ())), preferred_element_type=jnp.float32
            )
            scores = scores + bias
            weights = jnp.exp2(scores - jnp.max(scores, axis=-1, keepdims=True))
            values = jnp.concatenate([values, jnp.ones_like(values)], axis=1)
            mixed = jnp.dot(
                weights.astype(jnp.bfloat16), values, preferred_element_type=jnp.float32
            )
            mixed = (mixed[:, :HD] * (1.0 / mixed[:, HD:])).astype(jnp.bfloat16)
            for g, c in enumerate(columns):
                attended[pl.ds(row, BLOCK), c : c + HD] = mixed[g * BLOCK : (g + 1) * BLOCK]
        return carry

    lax.fori_loop(0, tokens // BLOCK, attend, 0)
    later_ref[...] = qkv[tokens:, q_width:]

    def out_block(place, carry):
        block = part ^ jnp.where(place == 0, 1, jnp.where(place == 1, 3, jnp.where(place == 2, 0, 2)))
        product = jnp.dot(
            attended[...], w_out[:, columns_of(block)], preferred_element_type=jnp.float32
        ).astype(jnp.bfloat16)

        @pl.when(place < 2)
        def _():
            send_ref[:, columns_of(place)] = product

        @pl.when(place >= 2)
        def _():
            keep_ref[:, columns_of(place - 2)] = product

        return carry

    lax.fori_loop(0, 4, out_block, 0)


def layer(base, part, row_start, own, other, beside, earlier, inverse_gain, weights):
    tokens, width = own.shape
    w_out = weights[3]
    q_width, features = w_out.shape
    kv_width = weights[1].shape[1]
    whole = pl.BlockSpec(memory_space=pltpu.VMEM)
    half = jax.ShapeDtypeStruct((tokens, 2 * width), jnp.bfloat16)
    return pl.pallas_call(
        lambda *refs: layer_kernel(base, *refs),
        in_specs=[pl.BlockSpec(memory_space=pltpu.SMEM)] + [whole] * 10,
        out_specs=[whole] * 3,
        out_shape=[half, half, jax.ShapeDtypeStruct((PROMPT, 2 * kv_width), jnp.bfloat16)],
        scratch_shapes=[
            pltpu.VMEM((tokens, features), jnp.bfloat16),
            pltpu.VMEM((tokens, 128), jnp.float32),
            pltpu.VMEM((tokens + PROMPT, q_width + 2 * kv_width), jnp.bfloat16),
            pltpu.VMEM((tokens, q_width), jnp.bfloat16),
        ],
        compiler_params=pltpu.CompilerParams(vmem_limit_bytes=28 * 2**20),
        cost_estimate=pl.CostEstimate(
            flops=COST * 2 * tokens * features * (2 * q_width + 2 * kv_width),
            bytes_accessed=1024,
            transcendentals=0,
        ),
        name="prefill_layer",
    )(part[None], row_start, own, other, beside, earlier, inverse_gain, *weights)


def unpack_kernel(cuts, used_ref, offset_ref, *refs):
    pieces, out_ref, held = refs[:-2], refs[-2], refs[-1]
    step = pl.program_id(0)

    @pl.when(step == 0)
    def _():
        for low, piece in zip(cuts, pieces):
            held[low : low + piece.shape[0], :] = piece[...]
        end = cuts[-1] + pieces[-1].shape[0]
        held[end:, :] = jnp.zeros((held.shape[0] - end, held.shape[1]), held.dtype)

    per_step, resp_len = out_ref.shape[:2]
    token = lax.broadcasted_iota(jnp.int32, (resp_len, 2 * resp_len), 0)
    place = lax.broadcasted_iota(jnp.int32, (resp_len, 2 * resp_len), 1)
    for k in range(per_step):
        offset = offset_ref[step * per_step + k]
        first = pl.multiple_of(offset // 16 * 16, 16)
        window = held[pl.ds(first, 2 * resp_len), :]
        mask = (place == token + (offset - first)) & (token < used_ref[step * per_step + k])
        mask = jnp.where(mask, 1.0, 0.0).astype(jnp.bfloat16)
        out_ref[k] = jnp.dot(mask, window, preferred_element_type=jnp.float32).astype(jnp.bfloat16)


def unpack(used, offset, pieces, cuts, resp_len):
    slots, width = used.shape[0], pieces[0].shape[1]
    per_step = 2 if slots % 2 == 0 else 1
    full = lambda piece: pl.BlockSpec(piece.shape, lambda s, *_: (0, 0))
    return pl.pallas_call(
        lambda *refs: unpack_kernel(cuts, *refs),
        grid_spec=pltpu.PrefetchScalarGridSpec(
            num_scalar_prefetch=2,
            grid=(slots // per_step,),
            in_specs=[full(piece) for piece in pieces],
            out_specs=pl.BlockSpec((per_step, resp_len, width), lambda s, *_: (s, 0, 0)),
            scratch_shapes=[pltpu.VMEM((cuts[-1] + pieces[-1].shape[0] + 2 * resp_len, width), jnp.bfloat16)],
        ),
        out_shape=jax.ShapeDtypeStruct((slots, resp_len, width), jnp.bfloat16),
        compiler_params=pltpu.CompilerParams(vmem_limit_bytes=24 * 2**20),
        name="unpack_slots",
    )(used, offset, *pieces)


def decode_kernel(length_ref, active_ref, query_ref, new_key_ref, new_value_ref, key_ref, value_ref, out_ref):
    row = pl.program_id(0)

    @pl.when(active_ref[row] == 0)
    def _():
        out_ref[...] = jnp.zeros_like(out_ref)

    @pl.when(active_ref[row] != 0)
    def _():
        scale = 1.0 / math.sqrt(HD)
        valid = PROMPT + length_ref[row]
        keys, values = key_ref[0], value_ref[0]
        nums = (((1,), (1,)), ((), ()))
        for head in range(query_ref.shape[1]):
            queries = query_ref[0, head]
            lanes = slice(head * HD, (head + 1) * HD)
            old = lax.dot_general(queries, keys[:, lanes], nums, preferred_element_type=jnp.float32)
            new = lax.dot_general(
                queries, new_key_ref[0, head], nums, preferred_element_type=jnp.float32
            )
            position = lax.broadcasted_iota(jnp.int32, old.shape, 1)
            old = jnp.where(position < valid, old * scale, NEG)
            step = lax.broadcasted_iota(jnp.int32, new.shape, 0) // (QH // KVH)
            new = jnp.where(lax.broadcasted_iota(jnp.int32, new.shape, 1) <= step, new * scale, NEG)
            top = jnp.maximum(
                jnp.max(old, axis=-1, keepdims=True), jnp.max(new, axis=-1, keepdims=True)
            )
            old_weights, new_weights = jnp.exp(old - top), jnp.exp(new - top)
            total = jnp.sum(old_weights, axis=-1, keepdims=True) + jnp.sum(
                new_weights, axis=-1, keepdims=True
            )
            mixed = jnp.dot(
                (old_weights / total).astype(jnp.bfloat16),
                values[:, lanes],
                preferred_element_type=jnp.float32,
            ) + jnp.dot(
                (new_weights / total).astype(jnp.bfloat16),
                new_value_ref[0, head],
                preferred_element_type=jnp.float32,
            )
            out_ref[0, head] = mixed.astype(jnp.bfloat16)


def decode_here(length, active, fresh, cache_keys, cache_values, steps):
    rows, cache_len, kv_width = cache_keys.shape
    heads = kv_width // HD
    group = QH // KVH
    q_width = heads * group * HD
    fresh = fresh.reshape(rows, steps, q_width + 2 * kv_width)
    queries = fresh[:, :, :q_width].reshape(rows, steps, heads, group, HD)
    queries = queries.transpose(0, 2, 1, 3, 4).reshape(rows, heads, steps * group, HD)
    new = fresh[:, :, q_width:].reshape(rows, steps, 2, heads, HD).transpose(2, 0, 3, 1, 4)
    new = jnp.pad(new, ((0, 0), (0, 0), (0, 0), (0, 16 - steps), (0, 0)))
    small = lambda n: pl.BlockSpec((1, heads, n, HD), lambda r, *_: (r, 0, 0, 0))
    cache = pl.BlockSpec((1, cache_len, kv_width), lambda r, *_: (r, 0, 0))
    out = pl.pallas_call(
        decode_kernel,
        grid_spec=pltpu.PrefetchScalarGridSpec(
            num_scalar_prefetch=2,
            grid=(rows,),
            in_specs=[small(steps * group), small(16), small(16), cache, cache],
            out_specs=small(steps * group),
        ),
        out_shape=jax.ShapeDtypeStruct((rows, heads, steps * group, HD), jnp.bfloat16),
        compiler_params=pltpu.CompilerParams(vmem_limit_bytes=16 * 2**20),
        cost_estimate=pl.CostEstimate(
            flops=4 * rows * cache_len * steps * q_width,
            bytes_accessed=8 * rows * cache_len * kv_width,
            transcendentals=0,
        ),
        name="decode_attention",
    )(length, active, queries, new[0], new[1], cache_keys, cache_values)
    out = out.reshape(rows, heads, steps, group, HD).transpose(0, 2, 1, 3, 4)
    return out.reshape(rows, steps * q_width)


def pick(mask, values):
    return jnp.dot(
        mask.astype(jnp.bfloat16), values, preferred_element_type=jnp.float32
    ).astype(jnp.bfloat16)


def two_shift_body(
    dest_slot,
    finished,
    lengths,
    cache_keys,
    cache_values,
    responses,
    dec_queries,
    new_keys,
    new_values,
    norm_gain,
    w_query,
    w_key,
    w_value,
    w_out,
):
    count = lax.axis_size("inst")
    here = lax.axis_index("inst")
    part = lax.axis_index("tp")
    tp = lax.axis_size("tp")
    reps = lax.axis_size("rep")
    rows, resp_len, width = responses.shape
    steps = dec_queries.shape[1]
    near, far = 1, count // 2
    cap = rows // 2
    full_cap = cap * resp_len

    def along(value, shift):
        return lax.ppermute(value, "inst", [(i, (i + shift) % count) for i in range(count)])

    def across(value):
        return lax.ppermute(value, "tp", [(i, i ^ 2) for i in range(tp)])

    def beside(value):
        return lax.ppermute(value, "tp", [(i, i ^ 1) for i in range(tp)])

    def ordered(value, *after):
        return lax.optimization_barrier((value,) + after)[0]

    slots = dest_slot.reshape(count, rows)
    shift = (slots // rows - jnp.arange(count)[:, None]) % count
    earlier = jnp.arange(rows)[None, :] < jnp.arange(rows)[:, None]

    def at(table, shift_back):
        return lax.dynamic_index_in_dim(table, (here - shift_back) % count, 0, keepdims=False)

    def rank_of(own_shift):
        same = own_shift[:, None] == own_shift[None, :]
        return jnp.sum((same & earlier).astype(jnp.int32), axis=1)

    own_slots, own_shift = at(slots, 0), at(shift, 0)
    own_rank = rank_of(own_shift)

    def layout(length, done, row_shift, which):
        used = jnp.where((row_shift == which) & (done == 1), length, 0)
        offset = jnp.sum(jnp.where(earlier, used[None, :], 0), axis=1)
        return used, offset, jnp.sum(used)

    def places(used, offset):
        inside = jnp.arange(resp_len)[None, :] < used[:, None]
        return jnp.where(inside, offset[:, None] + jnp.arange(resp_len)[None, :], -1)

    def starts(used, offset):
        token = jnp.arange(full_cap, dtype=jnp.int32)
        begun = (offset[None, :] <= token[:, None]) & (used[None, :] > 0)
        return jnp.max(jnp.where(begun, offset[None, :], 0), axis=1)[:, None]

    used_near, offset_near, total_near = layout(lengths, finished, own_shift, near)
    used_far, offset_far, total_far = layout(lengths, finished, own_shift, far)
    place_near = places(used_near, offset_near).reshape(1, rows * resp_len)
    place_far = places(used_far, offset_far).reshape(1, rows * resp_len)
    flat = responses.reshape(rows * resp_len, width)
    own_gain = lax.dynamic_slice_in_dim(norm_gain, part * width, width)


    def packed(place, low, high):
        token = jnp.arange(low, high, dtype=jnp.int32)[:, None]
        chosen = jnp.dot(
            (token == place).astype(jnp.bfloat16), flat, preferred_element_type=jnp.float32
        )
        return (chosen * own_gain).astype(jnp.bfloat16)

    fresh = jnp.concatenate([dec_queries, new_keys, new_values], axis=2)
    fresh = fresh.reshape(rows, -1)

    def slot_of(shift_back, row_rank, row_shift, which):
        source_slots = at(slots, shift_back)
        source_shift = at(shift, shift_back)
        local = jnp.where(source_shift == which, source_slots - here * rows, -1)
        hit = local[None, :] == jnp.arange(rows)[:, None]
        return hit

    def rank_mask(row_shift, row_rank, which):
        member = (row_shift == which)[:, None]
        return member & (row_rank[:, None] == jnp.arange(cap)[None, :])

    near_shift, far_shift = at(shift, near), at(shift, far)
    near_rank, far_rank = rank_of(near_shift), rank_of(far_shift)
    near_hit = slot_of(near, near_rank, near_shift, near)
    far_hit = slot_of(far, far_rank, far_shift, far)
    near_slot = jnp.any(near_hit[:, :, None] & rank_mask(near_shift, near_rank, near)[None], axis=1)
    far_slot = jnp.any(far_hit[:, :, None] & rank_mask(far_shift, far_rank, far)[None], axis=1)
    most = jnp.maximum(total_near, total_far)
    notes = jnp.concatenate(
        [lengths, finished, jnp.stack([most // resp_len, most % resp_len])]
    ).astype(jnp.bfloat16)

    def noted(values):
        block = jnp.pad(notes[None], ((0, 15), (0, values.shape[1] - notes.shape[0])))
        return jnp.concatenate([values, block], axis=0)

    def read(values):
        line = values[-16, : notes.shape[0]].astype(jnp.int32)
        return line[:rows], line[rows : 2 * rows], line[2 * rows] * resp_len + line[2 * rows + 1]

    own_near = rank_mask(own_shift, own_rank, near)
    own_far = rank_mask(own_shift, own_rank, far)
    away_near, away_far = noted(pick(near_slot.T, fresh)), noted(pick(far_slot.T, fresh))
    back_near, back_far = along(away_near, -near), along(away_far, -far)
    flat = ordered(flat, away_near, away_far)
    far_states = packed(place_far, 0, full_cap)
    flat = ordered(flat, far_states)
    near_states = packed(place_near, 0, full_cap)
    own_group = jnp.concatenate([own_near, own_far], axis=1)
    own_fresh = pick(own_group, jnp.concatenate([back_near[:cap], back_far[:cap]], axis=0))
    inverse_gain = (1.0 / norm_gain)[None]

    start_near = starts(used_near, offset_near)

    def arrived(meta_came, row_shift, which):
        return layout(meta_came[0], meta_came[1], row_shift, which)

    def by_slot(hit, values):
        return jnp.sum(jnp.where(hit, values[None], 0), axis=1)

    kv_width = w_key.shape[1] + w_value.shape[1]

    capacity = min(CAPACITY, full_cap)

    def cut(shares):
        marks = [0]
        for k in range(1, len(shares)):
            marks.append(round(capacity * sum(shares[:k]) / sum(shares) / BLOCK) * BLOCK)
        return marks + [capacity]

    none = jnp.zeros((PROMPT, kv_width), jnp.bfloat16)
    weights = (w_query, w_key, w_value, w_out)
    near_cuts, far_cuts = cut(NEAR_SHARES), cut(FAR_SHARES)
    near_parts = [near_states[a:b] for a, b in zip(near_cuts, near_cuts[1:])]
    near_others = [across(piece) for piece in near_parts]
    far_parts = [far_states[a:b] for a, b in zip(far_cuts, far_cuts[1:])]
    far_parts[0] = along(noted(far_parts[0]), far)
    from_far = read(far_parts[0])
    arrived_last = far_parts[0]
    far_parts[0] = far_parts[0][:-16]
    used_b, offset_b, _ = arrived(from_far, far_shift, far)
    start_far = starts(used_b, offset_b)
    lows = near_cuts[:-1] + far_cuts[:-1]
    first_far, last = len(near_parts), len(lows) - 1
    owns = near_parts + far_parts
    others, boths, cames = list(near_others), [], []
    sent, kept, crossed, chips, turned, done = [], [], [], [], [], []

    def after_kernel(value, c):
        return ordered(value, sent[c]) if 0 <= c < len(sent) else value

    def fetch(c):
        if first_far < c <= last:
            gone = owns[c - 1] if c - 1 > first_far else arrived_last
            owns[c] = along(ordered(owns[c], after_kernel(gone, c - 4)), far)

    def meet(c):
        if c == len(others):
            others.append(across(after_kernel(owns[c], c - 3)))
        other = after_kernel(others[c], c - 2)
        own = after_kernel(owns[c], c - 2)
        boths.append(jnp.concatenate([own, other], axis=1))
        cames.append(beside(boths[c]))

    def add(c):
        chips.append(after_kernel(crossed[c], c + 1))
        both = kept[c][:, width:].astype(jnp.float32) + chips[c][:, width:].astype(jnp.float32)
        both = both.astype(jnp.bfloat16)
        turned.append(across(both))
        return both

    def finish(c):
        got = after_kernel(turned[c], c + 3).astype(jnp.float32)
        both = kept[c][:, :width].astype(jnp.float32) + chips[c][:, :width].astype(jnp.float32)
        total = (both + got).astype(jnp.bfloat16)
        if c == 0:
            total = noted(total)
        done.append(along(total, near) if c < first_far else total)
        return total

    fetch(first_far + 1)
    meet(0)
    tail = none
    for c, low in enumerate(lows):
        before = [boths[0]] if c == 0 else [own_fresh] if c == 1 else []
        fetch(c + 3 if c + 3 > first_far + 1 else -1)
        if c < last:
            meet(c + 1)
            before.append(boths[c + 1])
        if c >= 2:
            before.append(add(c - 2))
        if c == 4:
            before.append(finish(0))
        if c == first_far:
            near_tail = tail
            tail = ordered(none, tail)
        tail = ordered(tail, *before)
        high = low + owns[c].shape[0]
        row_start = start_near if c < first_far else start_far
        send, keep, tail = layer(
            low,
            part,
            row_start[low:high],
            owns[c],
            others[c],
            cames[c],
            tail,
            inverse_gain,
            weights,
        )
        sent.append(send)
        kept.append(keep)
        crossed.append(beside(send))
    for c in range(len(chips), last + 1):
        gone = add(c)
    for c in range(len(done), last + 1):
        finish(c)
    decoded = decode_here(
        ordered(lengths, gone),
        1 - finished,
        own_fresh,
        cache_keys,
        cache_values,
        steps,
    )
    came_near = along(pick(own_near.T, decoded), near)
    came_far = along(pick(own_far.T, decoded), far)
    from_near, from_third = read(done[0]), read(back_near)
    for came in (from_near, from_far, from_third):
        most = jnp.maximum(most, came[2])
    most = ordered(most, gone)
    for k in range(1, reps):
        pairs = [(i, (i + k) % reps) for i in range(reps)]
        most = jnp.maximum(most, lax.ppermute(most, "rep", pairs))
    near_done, far_done = done[:first_far], done[first_far:]

    def overflow(near_x, far_x, near_kv, far_kv):
        def run(low, own, kv, row_start):
            other = across(own)
            came = beside(jnp.concatenate([own, other], axis=1))
            send, keep, _ = layer(
                low, part, row_start[low:], own, other, came, kv, inverse_gain, weights
            )
            chip = keep.astype(jnp.float32) + beside(send).astype(jnp.float32)
            got = across(chip[:, width:].astype(jnp.bfloat16))
            return (chip[:, :width] + got.astype(jnp.float32)).astype(jnp.bfloat16)

        near_more = along(run(capacity, near_x, near_kv, start_near), near)
        far_more = run(capacity, along(far_x, far), far_kv, start_far)
        return near_more, far_more

    def nothing(near_x, far_x, near_kv, far_kv):
        return jnp.zeros_like(near_x), jnp.zeros_like(far_x)

    if capacity < full_cap:
        near_more, far_more = lax.cond(
            most > capacity,
            overflow,
            nothing,
            near_states[capacity:],
            far_states[capacity:],
            near_tail,
            tail,
        )
        near_done, far_done = near_done + [near_more], far_done + [far_more]
        near_cuts, far_cuts = near_cuts + [full_cap], far_cuts + [full_cap]
    cuts = near_cuts[:-1] + [full_cap + cut_ for cut_ in far_cuts[:-1]]
    used_a, offset_a, _ = arrived(from_near, near_shift, near)
    near_used, far_used = by_slot(near_hit, used_a), by_slot(far_hit, used_b)
    near_offset, far_offset = by_slot(near_hit, offset_a), by_slot(far_hit, offset_b)
    offset = near_offset + jnp.where(far_used > 0, far_offset + full_cap, 0)
    prefilled = unpack(near_used + far_used, offset, near_done + far_done, cuts, resp_len)
    active_slot = jnp.concatenate([near_slot, far_slot], axis=1)
    decoded = pick(active_slot, jnp.concatenate([came_near, came_far], axis=0))
    return decoded.reshape(rows, steps, -1), prefilled


def place_rows(values, index, count):
    buffer = jnp.zeros((count,) + values.shape[1:], values.dtype)
    return buffer.at[index].set(values)


def decode_rows(queries, fresh_keys, fresh_values, old_keys, old_values, length):
    row_count, step_count, width = queries.shape
    heads_kv = old_keys.shape[2] // HD
    group_size = QH // KVH
    cache_len = old_keys.shape[1]
    score_scale = 1.0 / math.sqrt(HD)
    query_heads = queries.reshape(row_count, step_count, heads_kv, group_size, HD)
    key_heads = old_keys.reshape(row_count, cache_len, heads_kv, HD)
    value_heads = old_values.reshape(row_count, cache_len, heads_kv, HD)
    fresh_key_heads = fresh_keys.reshape(row_count, step_count, heads_kv, HD)
    fresh_value_heads = fresh_values.reshape(row_count, step_count, heads_kv, HD)
    old_scores = (
        jnp.einsum("rskgd,rpkd->rskgp", query_heads, key_heads, preferred_element_type=jnp.float32)
        * score_scale
    )
    new_scores = (
        jnp.einsum(
            "rskgd,rtkd->rskgt", query_heads, fresh_key_heads, preferred_element_type=jnp.float32
        )
        * score_scale
    )
    old_valid = jnp.arange(cache_len)[None, :] < PROMPT + length[:, None]
    step_index = jnp.arange(step_count)
    new_valid = step_index[None, :] <= step_index[:, None]
    old_scores = jnp.where(old_valid[:, None, None, None, :], old_scores, -1e30)
    new_scores = jnp.where(new_valid[None, :, None, None, :], new_scores, -1e30)
    top_score = jnp.maximum(
        jnp.max(old_scores, axis=-1, keepdims=True), jnp.max(new_scores, axis=-1, keepdims=True)
    )
    old_weights = jnp.exp(old_scores - top_score)
    new_weights = jnp.exp(new_scores - top_score)
    totals = jnp.sum(old_weights, axis=-1, keepdims=True) + jnp.sum(
        new_weights, axis=-1, keepdims=True
    )
    old_probs = (old_weights / totals).astype(jnp.bfloat16)
    new_probs = (new_weights / totals).astype(jnp.bfloat16)
    mixed = jnp.einsum(
        "rskgp,rpkd->rskgd", old_probs, value_heads, preferred_element_type=jnp.float32
    )
    mixed = mixed + jnp.einsum(
        "rskgt,rtkd->rskgd", new_probs, fresh_value_heads, preferred_element_type=jnp.float32
    )
    return mixed.astype(jnp.bfloat16).reshape(row_count, step_count, width)


def prefill_rows(states, length, norm_gain, w_query, w_key, w_value, w_out):
    row_count, resp_len, width = states.shape
    heads_kv = w_key.shape[1] // HD
    group_size = QH // KVH
    score_scale = 1.0 / math.sqrt(HD)
    states_f = states.astype(jnp.float32)
    mean_square = jnp.mean(states_f * states_f, axis=-1, keepdims=True)
    normed = (states_f * lax.rsqrt(mean_square + 1e-06) * norm_gain).astype(jnp.bfloat16)
    flat_rows = normed.reshape(row_count * resp_len, width)
    query_proj = jnp.dot(flat_rows, w_query, preferred_element_type=jnp.float32).astype(
        jnp.bfloat16
    )
    key_proj = jnp.dot(flat_rows, w_key, preferred_element_type=jnp.float32).astype(jnp.bfloat16)
    value_proj = jnp.dot(flat_rows, w_value, preferred_element_type=jnp.float32).astype(
        jnp.bfloat16
    )
    query_heads = query_proj.reshape(row_count, resp_len, heads_kv, group_size, HD)
    key_heads = key_proj.reshape(row_count, resp_len, heads_kv, HD)
    value_heads = value_proj.reshape(row_count, resp_len, heads_kv, HD)
    scores = (
        jnp.einsum("rqkgd,rpkd->rkgqp", query_heads, key_heads, preferred_element_type=jnp.float32)
        * score_scale
    )
    positions = jnp.arange(resp_len)
    causal = positions[None, :] <= positions[:, None]
    allowed = causal[None, :, :] & (positions[None, None, :] < length[:, None, None])
    scores = jnp.where(allowed[:, None, None], scores, -1e30)
    top_score = jnp.max(scores, axis=-1, keepdims=True)
    weights = jnp.exp(scores - top_score)
    pre_probs = (weights / jnp.sum(weights, axis=-1, keepdims=True)).astype(jnp.bfloat16)
    attended = jnp.einsum(
        "rkgqp,rpkd->rqkgd", pre_probs, value_heads, preferred_element_type=jnp.float32
    )
    attended = attended.astype(jnp.bfloat16).reshape(
        row_count * resp_len, heads_kv * group_size * HD
    )
    return jnp.dot(attended, w_out, preferred_element_type=jnp.float32)


def general_body(
    dest_slot,
    finished,
    lengths,
    cache_keys,
    cache_values,
    responses,
    dec_queries,
    new_keys,
    new_values,
    norm_gain,
    w_query,
    w_key,
    w_value,
    w_out,
):
    inst_count = lax.axis_size("inst")
    here_index = lax.axis_index("inst")
    row_count = finished.shape[0]
    slot_count = dest_slot.shape[0]
    per_target = max(2, 2 * row_count // inst_count)
    bucket_count = inst_count * per_target
    target = (dest_slot // row_count).reshape(inst_count, row_count)
    earlier = jnp.arange(row_count)[None, :] < jnp.arange(row_count)[:, None]
    same_target = target[:, :, None] == target[:, None, :]
    order_rank = jnp.sum(jnp.where(same_target & earlier[None], 1, 0), axis=2).astype(jnp.int32)
    bucket = (target * per_target + order_rank).reshape(slot_count)
    own_bucket = lax.dynamic_slice_in_dim(bucket, here_index * row_count, row_count)
    source = (
        jnp.zeros((slot_count,), jnp.int32)
        .at[dest_slot]
        .set(jnp.arange(slot_count, dtype=jnp.int32))
    )
    arrivals = lax.dynamic_slice_in_dim(source, here_index * row_count, row_count)
    incoming = arrivals // row_count * per_target + order_rank.reshape(slot_count)[arrivals]
    received = (
        lax.all_to_all(
            place_rows(responses, own_bucket, bucket_count),
            "inst",
            split_axis=0,
            concat_axis=0,
            tiled=True,
        ),
        lax.all_to_all(
            place_rows(finished, own_bucket, bucket_count),
            "inst",
            split_axis=0,
            concat_axis=0,
            tiled=True,
        ),
        lax.all_to_all(
            place_rows(lengths, own_bucket, bucket_count),
            "inst",
            split_axis=0,
            concat_axis=0,
            tiled=True,
        ),
    )
    slot_states = received[0][incoming]
    slot_done = received[1][incoming]
    slot_length = received[2][incoming]
    moved_caches = (
        lax.all_to_all(
            place_rows(cache_keys, own_bucket, bucket_count),
            "inst",
            split_axis=0,
            concat_axis=0,
            tiled=True,
        ),
        lax.all_to_all(
            place_rows(cache_values, own_bucket, bucket_count),
            "inst",
            split_axis=0,
            concat_axis=0,
            tiled=True,
        ),
    )
    decoded = decode_rows(
        dec_queries,
        new_keys,
        new_values,
        moved_caches[0][incoming],
        moved_caches[1][incoming],
        slot_length,
    )
    decoded = jnp.where(slot_done[:, None, None] == 0, decoded, jnp.zeros_like(decoded))
    states = lax.all_gather(slot_states, "tp", axis=2, tiled=True)
    partial_value = prefill_rows(states, slot_length, norm_gain, w_query, w_key, w_value, w_out)
    summed = lax.psum_scatter(
        partial_value.astype(jnp.bfloat16), "tp", scatter_dimension=1, tiled=True
    ).astype(jnp.float32)
    resp_len = states.shape[1]
    summed = summed.reshape(row_count, resp_len, -1)
    keep_mask = (jnp.arange(resp_len)[None, :] < slot_length[:, None]) & (slot_done[:, None] == 1)
    prefilled = jnp.where(keep_mask[:, :, None], summed, 0.0).astype(jnp.bfloat16)
    return (decoded, prefilled)


def body(*args):
    row_count = args[1].shape[0]
    inst_count = lax.axis_size("inst")
    two_groups = 2 * (2 * row_count // inst_count) == row_count and inst_count == 4
    if two_groups and lax.axis_size("tp") == 4:
        return two_shift_body(*args)
    return general_body(*args)


def solution(mesh):
    return jax.shard_map(
        body,
        mesh=mesh,
        in_specs=(
            P("rep"),
            P(("rep", "inst")),
            P(("rep", "inst")),
            P(("rep", "inst"), None, "tp"),
            P(("rep", "inst"), None, "tp"),
            P(("rep", "inst"), None, "tp"),
            P(("rep", "inst"), None, "tp"),
            P(("rep", "inst"), None, "tp"),
            P(("rep", "inst"), None, "tp"),
            P(),
            P(None, "tp"),
            P(None, "tp"),
            P(None, "tp"),
            P("tp", None),
        ),
        out_specs=(P(("rep", "inst"), None, "tp"), P(("rep", "inst"), None, "tp")),
        check_vma=False,
    )
```

profile of v0, /device:TPU:0, one launch (start us, length us, event | category | flops | bytes accessed | tf_op | source)
XLA Modules:
  0.0 171.7 jit_solution(11373599442933391282)
XLA Ops:
  0.7 0.9 reshape.349
  1.7 1.4 fusion.55
  3.1 0.7 broadcast_compare_fusion
  3.7 0.6 reduce_sum.121
  5.9 0.9 pad_maximum_fusion.6
  8.4 0.7 fusion.8
  9.1 5.0 %collective-permute-start.17 = (bf16[23,3072]{1,0:T(8,128)(2,1)}, bf16[23,3072]{1,0:T(8,128)(2,1)}, u32[]{:S(2)}, u32[]{:S(2)}) collective-permute-start(bf16[23,3072]{1,0:T(8,128)(2,1)} %get-tuple-element.174), channel_id=1, source_target_pairs={{0,12},{4,0},{8,4},{12,8},{1,13},{5,1},{9,5},{13,9},{2,14},{6,2},{... | collective-permute-start | bytes 423944 | tf_op jit(solution)/shard_map/ppermute | solution.py:320
  14.5 2.9 %multiply_convert_fusion.1 = bf16[896,768]{1,0:T(8,128)(2,1)S(1)} fusion(bf16[1792,768]{1,0:T(8,128)(2,1)S(1)} %bitcast.74, s32[1792]{0:T(1024)S(1)} %select_bitcast_fusion.1, f32[768]{0:T(1024)S(1)} %dynamic_slice.26), kind=kOutput, calls=%fused_computation.20 | convolution fusion | flops 2469232640 | bytes 4139008 | tf_op jit(solution)/shard_map/dot_general | solution.py:369
  17.5 2.9 %multiply_convert_fusion = bf16[896,768]{1,0:T(8,128)(2,1)S(1)} fusion(bf16[1792,768]{1,0:T(8,128)(2,1)S(1)} %bitcast.73, s32[1792]{0:T(1024)S(1)} %select_bitcast_fusion, f32[768]{0:T(1024)S(1)} %dynamic_slice.26), kind=kOutput, calls=%fused_computation.19 | convolution fusion | flops 2469232640 | bytes 4139008 | tf_op jit(solution)/shard_map/dot_general | solution.py:369
  20.5 1.6 collective-permute-start.14
  22.0 0.6 collective-permute-start.12
  22.6 0.8 fusion.56
  23.5 0.8 pad_maximum_fusion.5
  24.2 2.9 %collective-permute-start.10 = (bf16[272,768]{1,0:T(8,128)(2,1)}, bf16[272,768]{1,0:T(8,128)(2,1)}, u32[]{:S(2)}, u32[]{:S(2)}) collective-permute-start(bf16[272,768]{1,0:T(8,128)(2,1)} %pad_maximum_fusion.5), channel_id=1, source_target_pairs={{0,8},{4,12},{8,0},{12,4},{1,9},{5,13},{9,1},{13,5},{2,10},{6,14},... | collective-permute-start | bytes 1253384 | tf_op jit(solution)/shard_map/ppermute | solution.py:320
  27.4 0.7 slice.278
  28.2 0.8 slice.271.refs_1_
  29.1 0.7 slice_convert_fusion.2
  29.8 0.8 slice.282
  30.6 0.8 slice.283
  31.9 0.7 fusion.58
  33.9 11.0 %collective-permute-done.10 = bf16[272,768]{1,0:T(8,128)(2,1)} collective-permute-done((bf16[272,768]{1,0:T(8,128)(2,1)}, bf16[272,768]{1,0:T(8,128)(2,1)}, u32[]{:S(2)}, u32[]{:S(2)}) %collective-permute-start.10) | collective-permute-done | bytes 417824 | tf_op jit(solution)/shard_map/ppermute | solution.py:320
  45.0 1.0 slice.284.refs_2_
  46.0 1.6 collective-permute-start.19
  47.5 0.7 slice_convert_fusion.4
  48.2 1.0 pad_maximum_fusion.3
  49.6 0.8 copy.30.refs_1_
  50.4 0.8 copy.31.refs_1_
  51.2 0.8 copy.32.refs_1_
  51.9 0.6 fusion.59
  54.0 0.6 collective-permute-start.16
  54.7 16.9 %prefill_layer.9 = (bf16[320,1536]{1,0:T(8,128)(2,1)S(1)}, bf16[320,1536]{1,0:T(8,128)(2,1)S(1)}, bf16[128,512]{1,0:T(8,128)(2,1)S(1)}) custom-call(s32[1]{0:T(128)} %bitcast.8.refs_0_, s32[320,1]{1,0:T(8,128)S(1)} %slice.270.refs_1_, bf16[320,768]{1,0:T(8,128)(2,1)S(1)} %slice.280.refs_2_, bf16[320,768]{1,0:T(8,128)(2,1)S(1)} %collective-permute-done.12.refs_3_, ...), custom_call_target="tpu_custom_call" | custom-call | flops 15099494400 | bytes 1024 | tf_op jit(solution)/shard_map/prefill_layer/pallas_call | solution.py:147
  72.9 2.9 %collective-permute-start.15 = (bf16[192,768]{1,0:T(8,128)(2,1)S(1)}, bf16[192,768]{1,0:T(8,128)(2,1)S(1)}, u32[]{:S(2)}, u32[]{:S(2)}) collective-permute-start(bf16[192,768]{1,0:T(8,128)(2,1)S(1)} %copy-done.25), channel_id=1, source_target_pairs={{0,8},{4,12},{8,0},{12,4},{1,9},{5,13},{9,1},{13,5},{2,10},{6,14},... | collective-permute-start | bytes 884744 | tf_op jit(solution)/shard_map/ppermute | solution.py:320
  75.9 14.0 %prefill_layer.10 = (bf16[384,1536]{1,0:T(8,128)(2,1)S(1)}, bf16[384,1536]{1,0:T(8,128)(2,1)S(1)}, bf16[128,512]{1,0:T(8,128)(2,1)}) custom-call(s32[1]{0:T(128)} %bitcast.8.refs_0_, s32[384,1]{1,0:T(8,128)S(1)} %copy-done.14, bf16[384,768]{1,0:T(8,128)(2,1)S(1)} %slice.281.refs_2_, bf16[384,768]{1,0:T(8,128)(2,1)S(1)} %collective-permute-done.14.refs_3_, ...), custom_call_target="tpu_custom_call" | custom-call | flops 18119393280 | bytes 1024 | tf_op jit(solution)/shard_map/prefill_layer/pallas_call | solution.py:147
  89.9 1.6 collective-permute-start.20
  91.4 1.0 constant_dynamic-update-slice_fusion.3
  92.8 0.6 collective-permute-start.28
  93.5 9.3 %prefill_layer.11 = (bf16[256,1536]{1,0:T(8,128)(2,1)S(1)}, bf16[256,1536]{1,0:T(8,128)(2,1)S(1)}, bf16[128,512]{1,0:T(8,128)(2,1)S(1)}) custom-call(s32[1]{0:T(128)} %bitcast.8.refs_0_, s32[256,1]{1,0:T(8,128)S(1)} %copy-done.16, bf16[256,768]{1,0:T(8,128)(2,1)S(1)} %slice.284.refs_2_, bf16[256,768]{1,0:T(8,128)(2,1)S(1)} %copy-done.13, ...), custom_call_target="tpu_custom_call" | custom-call | flops 12079595520 | bytes 1024 | tf_op jit(solution)/shard_map/prefill_layer/pallas_call | solution.py:147
  103.5 1.1 add_convert_fusion.1
  104.6 1.5 collective-permute-start.33
  106.1 11.4 %prefill_layer.12 = (bf16[256,1536]{1,0:T(8,128)(2,1)}, bf16[256,1536]{1,0:T(8,128)(2,1)S(1)}, bf16[128,512]{1,0:T(8,128)(2,1)S(1)}) custom-call(s32[1]{0:T(128)} %bitcast.8.refs_0_, s32[256,1]{1,0:T(8,128)S(1)} %copy-done.15, bf16[256,768]{1,0:T(8,128)(2,1)} %collective-permute-done.11.refs_2_, bf16[256,768]{1,0:T(8,128)(2,1)S(1)} %collective-permute-done.22.refs_3_, ...), custom_call_target="tpu_custom_call" | custom-call | flops 12079595520 | bytes 1024 | tf_op jit(solution)/shard_map/prefill_layer/pallas_call | solution.py:147
  118.4 0.9 add_convert_fusion.7
  119.3 0.6 collective-permute-start.36
  119.9 8.2 %prefill_layer.13 = (bf16[192,1536]{1,0:T(8,128)(2,1)}, bf16[192,1536]{1,0:T(8,128)(2,1)S(1)}, bf16[128,512]{1,0:T(8,128)(2,1)}) custom-call(s32[1]{0:T(128)} %bitcast.8.refs_0_, s32[192,1]{1,0:T(8,128)S(1)} %copy-done.17, bf16[192,768]{1,0:T(8,128)(2,1)S(1)} %collective-permute-done.15.refs_2_, bf16[192,768]{1,0:T(8,128)(2,1)S(1)} %collective-permute-done.20.refs_3_, ...), custom_call_target="tpu_custom_call" | custom-call | flops 9059696640 | bytes 1024 | tf_op jit(solution)/shard_map/prefill_layer/pallas_call | solution.py:147
  128.1 5.6 %collective-permute-done.32.refs_2_ = bf16[336,768]{1,0:T(8,128)(2,1)S(1)} collective-permute-done((bf16[336,768]{1,0:T(8,128)(2,1)S(1)}, bf16[336,768]{1,0:T(8,128)(2,1)S(1)}, u32[]{:S(2)}, u32[]{:S(2)}) %collective-permute-start.32) | collective-permute-done | bytes 516128 | tf_op jit(solution)/shard_map/ppermute | solution.py:320
  133.8 0.8 copy-done.10
  134.9 0.6 fusion.60
  136.8 2.3 %add_convert_fusion = bf16[384,768]{1,0:T(8,128)(2,1)} fusion(bf16[384,768]{1,0:T(8,128)(2,1)} %collective-permute-done.33, bf16[384,1536]{1,0:T(8,128)(2,1)} %copy-done.23, bf16[384,1536]{1,0:T(8,128)(2,1)S(1)} %get-tuple-element.113), kind=kLoop, calls=%fused_computation.25 | loop fusion | flops 1769472 | bytes 2359296 | tf_op jit(solution)/shard_map/convert_element_type | solution.py:481
  139.1 1.8 %add_convert_fusion.5 = bf16[256,768]{1,0:T(8,128)(2,1)} fusion(bf16[256,1536]{1,0:T(8,128)(2,1)} %collective-permute-done.37, bf16[256,1536]{1,0:T(8,128)(2,1)S(1)} %get-tuple-element.129), kind=kLoop, calls=%fused_computation.31 | loop fusion | flops 786432 | bytes 1179648 | tf_op jit(solution)/shard_map/convert_element_type | solution.py:474
  141.5 1.8 %add_convert_fusion.9 = bf16[192,768]{1,0:T(8,128)(2,1)} fusion(bf16[192,1536]{1,0:T(8,128)(2,1)} %collective-permute-done.29, bf16[192,1536]{1,0:T(8,128)(2,1)S(1)} %get-tuple-element.122), kind=kLoop, calls=%fused_computation.35 | loop fusion | flops 589824 | bytes 884736 | tf_op jit(solution)/shard_map/convert_element_type | solution.py:474
  143.3 2.8 %collective-permute-start.35 = (s32[]{:T(128)}, s32[]{:T(128)}, u32[]{:S(2)}, u32[]{:S(2)}) collective-permute-start(s32[]{:T(128)} %max.18), channel_id=1, source_target_pairs={{0,16},{16,0},{1,17},{17,1},{2,18},{18,2},{3,19},{19,3},{4,20},{20... | collective-permute-start | bytes 20 | tf_op jit(solution)/shard_map/ppermute | solution.py:540
  146.1 0.8 collective-permute-done.35
  147.6 0.8 conditional.1
  147.6 0.7 broadcast.144
  148.4 1.5 collective-permute-start.39
  149.9 1.5 copy-done.3
  151.4 0.9 decode_attention.1
  152.7 4.1 %collective-permute-start.30 = (bf16[7,2048]{1,0:T(8,128)(2,1)S(1)}, bf16[7,2048]{1,0:T(8,128)(2,1)S(1)}, u32[]{:S(2)}, u32[]{:S(2)}) collective-permute-start(bf16[7,2048]{1,0:T(8,128)(2,1)S(1)} %convolution_convert_fusion.5), channel_id=1, source_target_pairs={{0,4},{4,8},{8,12},{12,0},{1,5},{5,9},{9,13},{13,1},{2,6},{6,10},{... | collective-permute-start | bytes 86024 | tf_op jit(solution)/shard_map/ppermute | solution.py:320
  157.1 1.3 collective-permute-start.31
  158.4 1.3 add_convert_fusion.6.refs_5_
  159.7 2.3 %collective-permute-done.31 = bf16[7,2048]{1,0:T(8,128)(2,1)S(1)} collective-permute-done((bf16[7,2048]{1,0:T(8,128)(2,1)S(1)}, bf16[7,2048]{1,0:T(8,128)(2,1)S(1)}, u32[]{:S(2)}, u32[]{:S(2)}) %collective-permute-start.31) | collective-permute-done | bytes 28704 | tf_op jit(solution)/shard_map/ppermute | solution.py:320
  162.1 0.7 reshape.358
  162.8 1.2 add_convert_fusion.8.refs_7_
  164.1 1.3 add_convert_fusion.4.refs_6_
  165.4 6.3 %unpack_slots.1 = bf16[14,128,768]{2,1,0:T(8,128)(2,1)} custom-call(s32[14]{0:T(128)S(1)} %get-tuple-element.167.refs_0_, s32[14]{0:T(128)S(1)} %get-tuple-element.166.refs_1_, bf16[336,768]{1,0:T(8,128)(2,1)S(1)} %copy-done.11, bf16[384,768]{1,0:T(8,128)(2,1)} %collective-permute-done.34.refs_3_, bf16[192,768]{1,0:T(8,128)(2,1)} %get-tuple-element.128.refs_4_, ...), custom_call_target="tpu_custom_call" | custom-call | tf_op jit(solution)/shard_map/unpack_slots/pallas_call | solution.py:195
  (202 shorter events, 8.6 us)
Async XLA Ops:
  0.6 13.6 %copy-start = (bf16[14,128,768]{2,1,0:T(8,128)(2,1)S(1)}, bf16[14,128,768]{2,1,0:T(8,128)(2,1)}, u32[]{:S(2)}) copy-start(bf16[14,128,768]{2,1,0:T(8,128)(2,1)} %param.21) | copy-start | bytes 8257540
  0.6 13.8 %copy-start.28 = (f32[3072]{0:T(1024)S(1)}, f32[3072]{0:T(1024)}, u32[]{:S(2)}) copy-start(f32[3072]{0:T(1024)} %param.25) | copy-start | bytes 36868
  1.7 5.5 %copy-start.34 = (s32[14]{0:T(128)}, s32[14]{0:T(128)S(1)}, u32[]{:S(2)}) copy-start(s32[14]{0:T(128)S(1)} %get-tuple-element.157) | copy-start | bytes 172
  1.7 27.3 %copy-start.36 = (pred[14]{0:T(512)(128)(4,1)}, pred[14]{0:T(512)(128)(4,1)S(1)}, u32[]{:S(2)}) copy-start(pred[14]{0:T(512)(128)(4,1)S(1)} %get-tuple-element.158) | copy-start | bytes 46
  3.7 25.3 %copy-start.38 = (pred[14]{0:T(512)(128)(4,1)}, pred[14]{0:T(512)(128)(4,1)S(1)}, u32[]{:S(2)}) copy-start(pred[14]{0:T(512)(128)(4,1)S(1)} %get-tuple-element.172) | copy-start | bytes 46
  7.1 21.9 %copy-start.40 = (s32[14]{0:T(128)}, s32[14]{0:T(128)S(1)}, u32[]{:S(2)}) copy-start(s32[14]{0:T(128)S(1)} %get-tuple-element.176) | copy-start | bytes 172
  9.1 20.0 %collective-permute-start.17 = (bf16[23,3072]{1,0:T(8,128)(2,1)}, bf16[23,3072]{1,0:T(8,128)(2,1)}, u32[]{:S(2)}, u32[]{:S(2)}) collective-permute-start(bf16[23,3072]{1,0:T(8,128)(2,1)} %get-tuple-element.174), channel_id=1, source_target_pairs={{0,12},{4,0},{8,4},{12,8},{1,13},{5,1},{9,5},{13,9},{2,14},{6,2},{... | collective-permute-start | bytes 423944 | tf_op jit(solution)/shard_map/ppermute | solution.py:320
  14.1 16.5 %collective-permute-start.18 = (bf16[23,3072]{1,0:T(8,128)(2,1)S(1)}, bf16[23,3072]{1,0:T(8,128)(2,1)}, u32[]{:S(2)}, u32[]{:S(2)}) collective-permute-start(bf16[23,3072]{1,0:T(8,128)(2,1)S(1)} %get-tuple-element.173), channel_id=1, source_target_pairs={{0,8},{4,12},{8,0},{12,4},{1,9},{5,13},{9,1},{13,5},{2,10},{6,14},... | collective-permute-start | bytes 423944 | tf_op jit(solution)/shard_map/ppermute | solution.py:320
  17.4 9.9 %copy-start.19 = (bf16[896,768]{1,0:T(8,128)(2,1)}, bf16[896,768]{1,0:T(8,128)(2,1)S(1)}, u32[]{:S(2)}) copy-start(bf16[896,768]{1,0:T(8,128)(2,1)S(1)} %multiply_convert_fusion.1) | copy-start | bytes 4128772
  20.4 7.7 %copy-start.20 = (bf16[896,768]{1,0:T(8,128)(2,1)}, bf16[896,768]{1,0:T(8,128)(2,1)S(1)}, u32[]{:S(2)}) copy-start(bf16[896,768]{1,0:T(8,128)(2,1)S(1)} %multiply_convert_fusion) | copy-start | bytes 4128772
  20.5 33.5 %collective-permute-start.14 = (bf16[384,768]{1,0:T(8,128)(2,1)S(1)}, bf16[384,768]{1,0:T(8,128)(2,1)S(1)}, u32[]{:S(2)}, u32[]{:S(2)}) collective-permute-start(bf16[384,768]{1,0:T(8,128)(2,1)S(1)} %slice.281.refs_2_), channel_id=1, source_target_pairs={{0,2},{1,3},{2,0},{3,1},{4,6},{5,7},{6,4},{7,5},{8,10},{9,11},{10,... | collective-permute-start | bytes 1769480 | tf_op jit(solution)/shard_map/ppermute | solution.py:323
  22.0 26.2 %collective-permute-start.12 = (bf16[320,768]{1,0:T(8,128)(2,1)S(1)}, bf16[320,768]{1,0:T(8,128)(2,1)S(1)}, u32[]{:S(2)}, u32[]{:S(2)}) collective-permute-start(bf16[320,768]{1,0:T(8,128)(2,1)S(1)} %slice.280.refs_2_), channel_id=1, source_target_pairs={{0,2},{1,3},{2,0},{3,1},{4,6},{5,7},{6,4},{7,5},{8,10},{9,11},{10,... | collective-permute-start | bytes 1474568 | tf_op jit(solution)/shard_map/ppermute | solution.py:323
  23.5 7.9 %copy-start.26 = (bf16[16,768]{1,0:T(8,128)(2,1)}, bf16[16,768]{1,0:T(8,128)(2,1)S(1)}, u32[]{:S(2)}) copy-start(bf16[16,768]{1,0:T(8,128)(2,1)S(1)} %pad.15) | copy-start | bytes 73732
  24.2 20.7 %collective-permute-start.10 = (bf16[272,768]{1,0:T(8,128)(2,1)}, bf16[272,768]{1,0:T(8,128)(2,1)}, u32[]{:S(2)}, u32[]{:S(2)}) collective-permute-start(bf16[272,768]{1,0:T(8,128)(2,1)} %pad_maximum_fusion.5), channel_id=1, source_target_pairs={{0,8},{4,12},{8,0},{12,4},{1,9},{5,13},{9,1},{13,5},{2,10},{6,14},... | collective-permute-start | bytes 1253384 | tf_op jit(solution)/shard_map/ppermute | solution.py:320
  27.2 27.4 %copy-start.29 = (f32[3072]{0:T(1024)}, f32[3072]{0:T(1024)S(1)}, u32[]{:S(2)}) copy-start(f32[3072]{0:T(1024)S(1)} %broadcast_divide_fusion) | copy-start | bytes 36868
  46.0 7.8 %copy-start.33 = (s32[14]{0:T(128)S(1)}, s32[14]{0:T(128)}, u32[]{:S(2)}) copy-start(s32[14]{0:T(128)} %copy-done.32) | copy-start | bytes 172
  46.0 25.7 %collective-permute-start.19 = (bf16[256,768]{1,0:T(8,128)(2,1)S(1)}, bf16[256,768]{1,0:T(8,128)(2,1)S(1)}, u32[]{:S(2)}, u32[]{:S(2)}) collective-permute-start(bf16[256,768]{1,0:T(8,128)(2,1)S(1)} %slice.284.refs_2_), channel_id=1, source_target_pairs={{0,2},{1,3},{2,0},{3,1},{4,6},{5,7},{6,4},{7,5},{8,10},{9,11},{10,... | collective-permute-start | bytes 1179656 | tf_op jit(solution)/shard_map/ppermute | solution.py:323
  47.5 24.8 %collective-permute-start.11 = (bf16[256,768]{1,0:T(8,128)(2,1)}, bf16[256,768]{1,0:T(8,128)(2,1)}, u32[]{:S(2)}, u32[]{:S(2)}) collective-permute-start(bf16[256,768]{1,0:T(8,128)(2,1)} %get-tuple-element.90), channel_id=1, source_target_pairs={{0,8},{4,12},{8,0},{12,4},{1,9},{5,13},{9,1},{13,5},{2,10},{6,14},... | collective-permute-start | bytes 1179656 | tf_op jit(solution)/shard_map/ppermute | solution.py:320
  49.3 5.3 %collective-permute-start.13 = (bf16[320,1536]{1,0:T(8,128)(2,1)}, bf16[320,1536]{1,0:T(8,128)(2,1)}, u32[]{:S(2)}, u32[]{:S(2)}) collective-permute-start(bf16[320,1536]{1,0:T(8,128)(2,1)} %pad_maximum_fusion.3), channel_id=1, source_target_pairs={{0,1},{1,0},{2,3},{3,2},{4,5},{5,4},{6,7},{7,6},{8,9},{9,8},{10,11... | collective-permute-start | bytes 2949128 | tf_op jit(solution)/shard_map/ppermute | solution.py:326
  51.9 2.7 %copy-start.42 = (bf16[3072,256]{1,0:T(8,128)(2,1)S(1)}, bf16[3072,256]{1,0:T(8,128)(2,1)}, u32[]{:S(2)}) copy-start(bf16[3072,256]{1,0:T(8,128)(2,1)} %refs_8_.9) | copy-start | bytes 4718596
  54.0 21.8 %collective-permute-start.16 = (bf16[384,1536]{1,0:T(8,128)(2,1)S(1)}, bf16[384,1536]{1,0:T(8,128)(2,1)S(1)}, u32[]{:S(2)}, u32[]{:S(2)}) collective-permute-start(bf16[384,1536]{1,0:T(8,128)(2,1)S(1)} %pad_maximum_fusion.2), channel_id=1, source_target_pairs={{0,1},{1,0},{2,3},{3,2},{4,5},{5,4},{6,7},{7,6},{8,9},{9,8},{10,11... | collective-permute-start | bytes 3538952 | tf_op jit(solution)/shard_map/ppermute | solution.py:326
  54.6 21.2 %slice-start = ((s8[6291456]{0:T(1024)(128)(4,1)}), s8[4194304]{0:T(1024)(128)(4,1)S(1)}, s32[]{:S(2)}) async-start(s8[6291456]{0:T(1024)(128)(4,1)} %bitcast.94), calls=%async_computation | async-start | bytes 8388608
  54.6 21.2 %slice-start.4 = ((s8[6291456]{0:T(1024)(128)(4,1)}), s8[4194304]{0:T(1024)(128)(4,1)S(1)}, s32[]{:S(2)}) async-start(s8[6291456]{0:T(1024)(128)(4,1)} %bitcast.98), calls=%async_computation.4 | async-start | bytes 8388608
  54.6 21.2 %slice-start.1 = ((s8[6291456]{0:T(1024)(128)(4,1)}), s8[2097152]{0:T(1024)(128)(4,1)S(1)}, s32[]{:S(2)}) async-start(s8[6291456]{0:T(1024)(128)(4,1)} %bitcast.94), calls=%async_computation.1 | async-start | bytes 4194304
  54.6 21.2 %slice-start.5 = ((s8[6291456]{0:T(1024)(128)(4,1)}), s8[2097152]{0:T(1024)(128)(4,1)S(1)}, s32[]{:S(2)}) async-start(s8[6291456]{0:T(1024)(128)(4,1)} %bitcast.98), calls=%async_computation.5 | async-start | bytes 4194304
  54.6 21.2 %copy-start.44 = (bf16[3072,256]{1,0:T(8,128)(2,1)S(1)}, bf16[3072,256]{1,0:T(8,128)(2,1)}, u32[]{:S(2)}) copy-start(bf16[3072,256]{1,0:T(8,128)(2,1)} %refs_9_.9) | copy-start | bytes 4718596
  71.6 4.3 %copy-start.14 = (s32[384,1]{1,0:T(8,128)S(1)}, s32[384,1]{1,0:T(8,128)}, u32[]{:S(2)}) copy-start(s32[384,1]{1,0:T(8,128)} %slice.271.refs_1_) | copy-start | bytes 4612
  71.6 4.3 %copy-start.30 = (f32[3072]{0:T(1024)S(1)}, f32[3072]{0:T(1024)}, u32[]{:S(2)}) copy-start(f32[3072]{0:T(1024)} %copy-done.29) | copy-start | bytes 36868
  71.6 21.1 %collective-permute-start.23 = (bf16[320,1536]{1,0:T(8,128)(2,1)S(1)}, bf16[320,1536]{1,0:T(8,128)(2,1)S(1)}, u32[]{:S(2)}, u32[]{:S(2)}) collective-permute-start(bf16[320,1536]{1,0:T(8,128)(2,1)S(1)} %get-tuple-element.93), channel_id=1, source_target_pairs={{0,1},{1,0},{2,3},{3,2},{4,5},{5,4},{6,7},{7,6},{8,9},{9,8},{10,11... | collective-permute-start | bytes 2949128 | tf_op jit(solution)/shard_map/ppermute | solution.py:326
  71.7 4.1 %copy-start.12 = (bf16[256,768]{1,0:T(8,128)(2,1)}, bf16[256,768]{1,0:T(8,128)(2,1)S(1)}, u32[]{:S(2)}) copy-start(bf16[256,768]{1,0:T(8,128)(2,1)S(1)} %collective-permute-done.19.refs_3_) | copy-start | bytes 1179652
  71.8 21.6 %collective-permute-start.21 = (bf16[256,1536]{1,0:T(8,128)(2,1)S(1)}, bf16[256,1536]{1,0:T(8,128)(2,1)S(1)}, u32[]{:S(2)}, u32[]{:S(2)}) collective-permute-start(bf16[256,1536]{1,0:T(8,128)(2,1)S(1)} %constant_dynamic-update-slice_fusion), channel_id=1, source_target_pairs={{0,1},{1,0},{2,3},{3,2},{4,5},{5,4},{6,7},{7,6},{8,9},{9,8},{10,11... | collective-permute-start | bytes 2359304 | tf_op jit(solution)/shard_map/ppermute | solution.py:326
  72.3 20.1 %collective-permute-start.22 = (bf16[256,768]{1,0:T(8,128)(2,1)}, bf16[256,768]{1,0:T(8,128)(2,1)S(1)}, u32[]{:S(2)}, u32[]{:S(2)}) collective-permute-start(bf16[256,768]{1,0:T(8,128)(2,1)} %collective-permute-done.11.refs_2_), channel_id=1, source_target_pairs={{0,2},{1,3},{2,0},{3,1},{4,6},{5,7},{6,4},{7,5},{8,10},{9,11},{10,... | collective-permute-start | bytes 1179656 | tf_op jit(solution)/shard_map/ppermute | solution.py:323
  72.9 17.0 %collective-permute-start.15 = (bf16[192,768]{1,0:T(8,128)(2,1)S(1)}, bf16[192,768]{1,0:T(8,128)(2,1)S(1)}, u32[]{:S(2)}, u32[]{:S(2)}) collective-permute-start(bf16[192,768]{1,0:T(8,128)(2,1)S(1)} %copy-done.25), channel_id=1, source_target_pairs={{0,8},{4,12},{8,0},{12,4},{1,9},{5,13},{9,1},{13,5},{2,10},{6,14},... | collective-permute-start | bytes 884744 | tf_op jit(solution)/shard_map/ppermute | solution.py:320
  89.8 13.6 %collective-permute-start.26 = (bf16[384,1536]{1,0:T(8,128)(2,1)S(1)}, bf16[384,1536]{1,0:T(8,128)(2,1)S(1)}, u32[]{:S(2)}, u32[]{:S(2)}) collective-permute-start(bf16[384,1536]{1,0:T(8,128)(2,1)S(1)} %get-tuple-element.100), channel_id=1, source_target_pairs={{0,1},{1,0},{2,3},{3,2},{4,5},{5,4},{6,7},{7,6},{8,9},{9,8},{10,11... | collective-permute-start | bytes 3538952 | tf_op jit(solution)/shard_map/ppermute | solution.py:326
  89.8 3.6 %copy-start.13 = (bf16[256,768]{1,0:T(8,128)(2,1)S(1)}, bf16[256,768]{1,0:T(8,128)(2,1)}, u32[]{:S(2)}) copy-start(bf16[256,768]{1,0:T(8,128)(2,1)} %copy-done.12) | copy-start | bytes 1179652
  89.8 3.6 %copy-start.16 = (s32[256,1]{1,0:T(8,128)S(1)}, s32[256,1]{1,0:T(8,128)}, u32[]{:S(2)}) copy-start(s32[256,1]{1,0:T(8,128)} %copy.30.refs_1_) | copy-start | bytes 3076
  89.9 13.1 %collective-permute-start.20 = (bf16[192,768]{1,0:T(8,128)(2,1)S(1)}, bf16[192,768]{1,0:T(8,128)(2,1)S(1)}, u32[]{:S(2)}, u32[]{:S(2)}) collective-permute-start(bf16[192,768]{1,0:T(8,128)(2,1)S(1)} %collective-permute-done.15.refs_2_), channel_id=1, source_target_pairs={{0,2},{1,3},{2,0},{3,1},{4,6},{5,7},{6,4},{7,5},{8,10},{9,11},{10,... | collective-permute-start | bytes 884744 | tf_op jit(solution)/shard_map/ppermute | solution.py:323
  92.5 13.6 %collective-permute-start.25 = (bf16[256,1536]{1,0:T(8,128)(2,1)S(1)}, bf16[256,1536]{1,0:T(8,128)(2,1)S(1)}, u32[]{:S(2)}, u32[]{:S(2)}) collective-permute-start(bf16[256,1536]{1,0:T(8,128)(2,1)S(1)} %constant_dynamic-update-slice_fusion.2), channel_id=1, source_target_pairs={{0,1},{1,0},{2,3},{3,2},{4,5},{5,4},{6,7},{7,6},{8,9},{9,8},{10,11... | collective-permute-start | bytes 2359304 | tf_op jit(solution)/shard_map/ppermute | solution.py:326
  92.8 24.7 %collective-permute-start.28 = (bf16[320,768]{1,0:T(8,128)(2,1)S(1)}, bf16[320,768]{1,0:T(8,128)(2,1)S(1)}, u32[]{:S(2)}, u32[]{:S(2)}) collective-permute-start(bf16[320,768]{1,0:T(8,128)(2,1)S(1)} %add_convert_fusion.3), channel_id=1, source_target_pairs={{0,2},{1,3},{2,0},{3,1},{4,6},{5,7},{6,4},{7,5},{8,10},{9,11},{10,... | collective-permute-start | bytes 1474568 | tf_op jit(solution)/shard_map/ppermute | solution.py:323
  102.8 15.6 %copy-start.4 = (bf16[256,1536]{1,0:T(8,128)(2,1)}, bf16[256,1536]{1,0:T(8,128)(2,1)S(1)}, u32[]{:S(2)}) copy-start(bf16[256,1536]{1,0:T(8,128)(2,1)S(1)} %get-tuple-element.117) | copy-start | bytes 2359300
  102.8 3.3 %copy-start.15 = (s32[256,1]{1,0:T(8,128)S(1)}, s32[256,1]{1,0:T(8,128)}, u32[]{:S(2)}) copy-start(s32[256,1]{1,0:T(8,128)} %copy.31.refs_1_) | copy-start | bytes 3076
  102.8 15.6 %collective-permute-start.27 = (bf16[256,1536]{1,0:T(8,128)(2,1)S(1)}, bf16[256,1536]{1,0:T(8,128)(2,1)S(1)}, u32[]{:S(2)}, u32[]{:S(2)}) collective-permute-start(bf16[256,1536]{1,0:T(8,128)(2,1)S(1)} %get-tuple-element.109), channel_id=1, source_target_pairs={{0,1},{1,0},{2,3},{3,2},{4,5},{5,4},{6,7},{7,6},{8,9},{9,8},{10,11... | collective-permute-start | bytes 2359304 | tf_op jit(solution)/shard_map/ppermute | solution.py:326
  103.0 16.9 %collective-permute-start.24 = (bf16[192,1536]{1,0:T(8,128)(2,1)S(1)}, bf16[192,1536]{1,0:T(8,128)(2,1)S(1)}, u32[]{:S(2)}, u32[]{:S(2)}) collective-permute-start(bf16[192,1536]{1,0:T(8,128)(2,1)S(1)} %constant_dynamic-update-slice_fusion.4), channel_id=1, source_target_pairs={{0,1},{1,0},{2,3},{3,2},{4,5},{5,4},{6,7},{7,6},{8,9},{9,8},{10,11... | collective-permute-start | bytes 1769480 | tf_op jit(solution)/shard_map/ppermute | solution.py:326
  104.6 32.2 %collective-permute-start.33 = (bf16[384,768]{1,0:T(8,128)(2,1)}, bf16[384,768]{1,0:T(8,128)(2,1)}, u32[]{:S(2)}, u32[]{:S(2)}) collective-permute-start(bf16[384,768]{1,0:T(8,128)(2,1)} %add_convert_fusion.1), channel_id=1, source_target_pairs={{0,2},{1,3},{2,0},{3,1},{4,6},{5,7},{6,4},{7,5},{8,10},{9,11},{10,... | collective-permute-start | bytes 1769480 | tf_op jit(solution)/shard_map/ppermute | solution.py:323
  117.5 21.6 %copy-start.6 = (bf16[256,1536]{1,0:T(8,128)(2,1)}, bf16[256,1536]{1,0:T(8,128)(2,1)S(1)}, u32[]{:S(2)}) copy-start(bf16[256,1536]{1,0:T(8,128)(2,1)S(1)} %get-tuple-element.129) | copy-start | bytes 2359300
  117.5 21.6 %collective-permute-start.37 = (bf16[256,1536]{1,0:T(8,128)(2,1)}, bf16[256,1536]{1,0:T(8,128)(2,1)}, u32[]{:S(2)}, u32[]{:S(2)}) collective-permute-start(bf16[256,1536]{1,0:T(8,128)(2,1)} %get-tuple-element.118), channel_id=1, source_target_pairs={{0,1},{1,0},{2,3},{3,2},{4,5},{5,4},{6,7},{7,6},{8,9},{9,8},{10,11... | collective-permute-start | bytes 2359304 | tf_op jit(solution)/shard_map/ppermute | solution.py:326
  118.3 15.5 %collective-permute-start.32 = (bf16[336,768]{1,0:T(8,128)(2,1)S(1)}, bf16[336,768]{1,0:T(8,128)(2,1)S(1)}, u32[]{:S(2)}, u32[]{:S(2)}) collective-permute-start(bf16[336,768]{1,0:T(8,128)(2,1)S(1)} %pad_maximum_fusion.4), channel_id=1, source_target_pairs={{0,4},{4,8},{8,12},{12,0},{1,5},{5,9},{9,13},{13,1},{2,6},{6,10},{... | collective-permute-start | bytes 1548296 | tf_op jit(solution)/shard_map/ppermute | solution.py:320
  118.4 9.8 %copy-start.24 = (bf16[256,1536]{1,0:T(8,128)(2,1)}, bf16[256,1536]{1,0:T(8,128)(2,1)S(1)}, u32[]{:S(2)}) copy-start(bf16[256,1536]{1,0:T(8,128)(2,1)S(1)} %collective-permute-done.27) | copy-start | bytes 2359300
  119.3 37.7 %collective-permute-start.36 = (bf16[256,768]{1,0:T(8,128)(2,1)}, bf16[256,768]{1,0:T(8,128)(2,1)}, u32[]{:S(2)}, u32[]{:S(2)}) collective-permute-start(bf16[256,768]{1,0:T(8,128)(2,1)} %add_convert_fusion.7), channel_id=1, source_target_pairs={{0,2},{1,3},{2,0},{3,1},{4,6},{5,7},{6,4},{7,5},{8,10},{9,11},{10,... | collective-permute-start | bytes 1179656 | tf_op jit(solution)/shard_map/ppermute | solution.py:323
  119.9 14.7 %copy-start.35 = (s32[14]{0:T(128)S(1)}, s32[14]{0:T(128)}, u32[]{:S(2)}) copy-start(s32[14]{0:T(128)} %copy-done.34) | copy-start | bytes 172
  128.1 13.4 %copy-start.8 = (bf16[192,1536]{1,0:T(8,128)(2,1)}, bf16[192,1536]{1,0:T(8,128)(2,1)S(1)}, u32[]{:S(2)}) copy-start(bf16[192,1536]{1,0:T(8,128)(2,1)S(1)} %get-tuple-element.122) | copy-start | bytes 1769476
  128.1 13.4 %collective-permute-start.29 = (bf16[192,1536]{1,0:T(8,128)(2,1)}, bf16[192,1536]{1,0:T(8,128)(2,1)}, u32[]{:S(2)}, u32[]{:S(2)}) collective-permute-start(bf16[192,1536]{1,0:T(8,128)(2,1)} %get-tuple-element.123), channel_id=1, source_target_pairs={{0,1},{1,0},{2,3},{3,2},{4,5},{5,4},{6,7},{7,6},{8,9},{9,8},{10,11... | collective-permute-start | bytes 1769480 | tf_op jit(solution)/shard_map/ppermute | solution.py:326
  139.1 8.5 %copy-start.31 = (f32[3072]{0:T(1024)S(1)}, f32[3072]{0:T(1024)}, u32[]{:S(2)}) copy-start(f32[3072]{0:T(1024)} %copy-done.29) | copy-start | bytes 36868
  139.1 26.2 %collective-permute-start.34 = (bf16[384,768]{1,0:T(8,128)(2,1)}, bf16[384,768]{1,0:T(8,128)(2,1)}, u32[]{:S(2)}, u32[]{:S(2)}) collective-permute-start(bf16[384,768]{1,0:T(8,128)(2,1)} %add_convert_fusion), channel_id=1, source_target_pairs={{0,4},{4,8},{8,12},{12,0},{1,5},{5,9},{9,13},{13,1},{2,6},{6,10},{... | collective-permute-start | bytes 1769480 | tf_op jit(solution)/shard_map/ppermute | solution.py:320
  140.9 23.1 %collective-permute-start.38 = (bf16[256,768]{1,0:T(8,128)(2,1)}, bf16[256,768]{1,0:T(8,128)(2,1)}, u32[]{:S(2)}, u32[]{:S(2)}) collective-permute-start(bf16[256,768]{1,0:T(8,128)(2,1)} %add_convert_fusion.5), channel_id=1, source_target_pairs={{0,2},{1,3},{2,0},{3,1},{4,6},{5,7},{6,4},{7,5},{8,10},{9,11},{10,... | collective-permute-start | bytes 1179656 | tf_op jit(solution)/shard_map/ppermute | solution.py:323
  143.3 3.6 %collective-permute-start.35 = (s32[]{:T(128)}, s32[]{:T(128)}, u32[]{:S(2)}, u32[]{:S(2)}) collective-permute-start(s32[]{:T(128)} %max.18), channel_id=1, source_target_pairs={{0,16},{16,0},{1,17},{17,1},{2,18},{18,2},{3,19},{19,3},{4,20},{20... | collective-permute-start | bytes 20 | tf_op jit(solution)/shard_map/ppermute | solution.py:540
  148.4 14.4 %collective-permute-start.39 = (bf16[192,768]{1,0:T(8,128)(2,1)}, bf16[192,768]{1,0:T(8,128)(2,1)}, u32[]{:S(2)}, u32[]{:S(2)}) collective-permute-start(bf16[192,768]{1,0:T(8,128)(2,1)} %add_convert_fusion.9), channel_id=1, source_target_pairs={{0,2},{1,3},{2,0},{3,1},{4,6},{5,7},{6,4},{7,5},{8,10},{9,11},{10,... | collective-permute-start | bytes 884744 | tf_op jit(solution)/shard_map/ppermute | solution.py:323
  151.4 5.3 %copy-start.39 = (pred[14]{0:T(512)(128)(4,1)S(1)}, pred[14]{0:T(512)(128)(4,1)}, u32[]{:S(2)}) copy-start(pred[14]{0:T(512)(128)(4,1)} %copy-done.38) | copy-start | bytes 46
  151.4 7.0 %copy-start.5 = (bf16[256,1536]{1,0:T(8,128)(2,1)S(1)}, bf16[256,1536]{1,0:T(8,128)(2,1)}, u32[]{:S(2)}) copy-start(bf16[256,1536]{1,0:T(8,128)(2,1)} %copy-done.4) | copy-start | bytes 2359300
  152.3 10.5 %copy-start.9 = (bf16[192,1536]{1,0:T(8,128)(2,1)S(1)}, bf16[192,1536]{1,0:T(8,128)(2,1)}, u32[]{:S(2)}) copy-start(bf16[192,1536]{1,0:T(8,128)(2,1)} %copy-done.8) | copy-start | bytes 1769476
  152.7 7.0 %collective-permute-start.30 = (bf16[7,2048]{1,0:T(8,128)(2,1)S(1)}, bf16[7,2048]{1,0:T(8,128)(2,1)S(1)}, u32[]{:S(2)}, u32[]{:S(2)}) collective-permute-start(bf16[7,2048]{1,0:T(8,128)(2,1)S(1)} %convolution_convert_fusion.5), channel_id=1, source_target_pairs={{0,4},{4,8},{8,12},{12,0},{1,5},{5,9},{9,13},{13,1},{2,6},{6,10},{... | collective-permute-start | bytes 86024 | tf_op jit(solution)/shard_map/ppermute | solution.py:320
  157.0 7.0 %copy-start.7 = (bf16[256,1536]{1,0:T(8,128)(2,1)S(1)}, bf16[256,1536]{1,0:T(8,128)(2,1)}, u32[]{:S(2)}) copy-start(bf16[256,1536]{1,0:T(8,128)(2,1)} %copy-done.6) | copy-start | bytes 2359300
  157.1 4.9 %collective-permute-start.31 = (bf16[7,2048]{1,0:T(8,128)(2,1)S(1)}, bf16[7,2048]{1,0:T(8,128)(2,1)S(1)}, u32[]{:S(2)}, u32[]{:S(2)}) collective-permute-start(bf16[7,2048]{1,0:T(8,128)(2,1)S(1)} %convolution_convert_fusion.4), channel_id=1, source_target_pairs={{0,8},{4,12},{8,0},{12,4},{1,9},{5,13},{9,1},{13,5},{2,10},{6,14},... | collective-permute-start | bytes 86024 | tf_op jit(solution)/shard_map/ppermute | solution.py:320
  165.4 6.3 %copy-start.1 = (bf16[14,128,768]{2,1,0:T(8,128)(2,1)S(1)}, bf16[14,128,768]{2,1,0:T(8,128)(2,1)}, u32[]{:S(2)}) copy-start(bf16[14,128,768]{2,1,0:T(8,128)(2,1)} %param.21) | copy-start | bytes 8257540
  (14 other events, 23.4 us)
where the time goes:
time: 175 us; the launch traced here: 172 us
  Pallas kernels  67 us (38%)
  starting transfers between devices  31.8 us (18%)
  other arithmetic  22.1 us (13%)
  waiting for transfers between devices  19.8 us (11%)
  local copies, waits for them, and re-layouts  16.5 us (9%)
  between operations  7.36 us (4%)
  matrix products  7.12 us (4%)
    pallas_call x5, Pallas kernels, layer(): pl.pallas_call(lambda *refs: layer_kernel(base, *refs), in_specs=[pl.Bloc...  59.8 us
    ppermute x9, waiting for transfers between devices, along(): lax.ppermute(value, 'inst', [(i, (i + shift) % count) for i in range(coun...  18.9 us
    ppermute x9, starting transfers between devices, along(): lax.ppermute(value, 'inst', [(i, (i + shift) % count) for i in range(coun...  16.4 us
    ppermute x10, starting transfers between devices, across(): return lax.ppermute(value, 'tp', [(i, i ^ 2) for i in range(tp)])  10.5 us
    pallas_call x1, Pallas kernels, unpack(): pl.pallas_call(lambda *refs: unpack_kernel(cuts, *refs), grid_spec=pltpu....  6.28 us
    convert_element_type x5, other arithmetic, finish(): total = (both + got).astype(jnp.bfloat16)  6.25 us
    convert_element_type x5, other arithmetic, add(): both = both.astype(jnp.bfloat16)  5.78 us
    dot_general x2, matrix products, packed(): jnp.dot((token == place).astype(jnp.bfloat16), flat, preferred_element_ty...  5.76 us
  transfers between devices with their start and end apart: 30, of which 4 were waited for; matrix products, arithmetic and copies ran while one was open for 21% of the time, Pallas kernels for 35%

commit v1 on v0

--- a/solution.py
+++ b/solution.py
@@ -90,7 +90,12 @@
         row = pl.multiple_of(b * BLOCK, BLOCK)
         query_pos = base + row + lax.broadcasted_iota(jnp.int32, shape, 0)
         key_pos = base + row - PROMPT + lax.broadcasted_iota(jnp.int32, shape, 1)
-        allowed = (key_pos >= start_ref[pl.ds(row, BLOCK), :]) & (key_pos <= query_pos)
+        token = base + row + lax.broadcasted_iota(jnp.int32, (BLOCK, 1), 0)
+        start = jnp.zeros((BLOCK, 1), jnp.int32)
+        for r in range(start_ref.shape[0]):
+            begin = start_ref[r]
+            start = jnp.where(token >= begin, jnp.maximum(start, begin), start)
+        allowed = (key_pos >= start) & (key_pos <= query_pos)
         bias = jnp.where(allowed, 0.0, NEG)
         bias = jnp.concatenate([bias] * group_size, axis=0)
         query_rows = pl.ds(pl.multiple_of(row + PROMPT, BLOCK), BLOCK)
@@ -146,7 +151,7 @@
     half = jax.ShapeDtypeStruct((tokens, 2 * width), jnp.bfloat16)
     return pl.pallas_call(
         lambda *refs: layer_kernel(base, *refs),
-        in_specs=[pl.BlockSpec(memory_space=pltpu.SMEM)] + [whole] * 10,
+        in_specs=[pl.BlockSpec(memory_space=pltpu.SMEM)] * 2 + [whole] * 9,
         out_specs=[whole] * 3,
         out_shape=[half, half, jax.ShapeDtypeStruct((PROMPT, 2 * kv_width), jnp.bfloat16)],
         scratch_shapes=[
@@ -207,8 +212,12 @@
     )(used, offset, *pieces)
 
 
-def decode_kernel(length_ref, active_ref, query_ref, new_key_ref, new_value_ref, key_ref, value_ref, out_ref):
+def decode_kernel(length_ref, active_ref, fresh_ref, key_ref, value_ref, out_ref):
     row = pl.program_id(0)
+    group, kv_width = QH // KVH, key_ref.shape[2]
+    q_width = group * kv_width
+    steps = out_ref.shape[2] // q_width
+    stride = q_width + 2 * kv_width
 
     @pl.when(active_ref[row] == 0)
     def _():
@@ -220,16 +229,25 @@
         valid = PROMPT + length_ref[row]
         keys, values = key_ref[0], value_ref[0]
         nums = (((1,), (1,)), ((), ()))
-        for head in range(query_ref.shape[1]):
-            queries = query_ref[0, head]
+
+        def stacked(starts):
+            rows = [fresh_ref[0, :, start : start + HD] for start in starts]
+            if len(rows) < 8:
+                rows.append(jnp.zeros((8 - len(rows), HD), jnp.float32))
+            return jnp.concatenate(rows, axis=0).astype(jnp.bfloat16)
+
+        for head in range(kv_width // HD):
+            order = [(t, head * group + g) for t in range(steps) for g in range(group)]
+            queries = stacked([t * stride + h * HD for t, h in order])
+            first = q_width + head * HD
+            new_keys = stacked([t * stride + first for t in range(steps)])
+            new_values = stacked([t * stride + first + kv_width for t in range(steps)])
             lanes = slice(head * HD, (head + 1) * HD)
             old = lax.dot_general(queries, keys[:, lanes], nums, preferred_element_type=jnp.float32)
-            new = lax.dot_general(
-                queries, new_key_ref[0, head], nums, preferred_element_type=jnp.float32
-            )
+            new = lax.dot_general(queries, new_keys, nums, preferred_element_type=jnp.float32)
             position = lax.broadcasted_iota(jnp.int32, old.shape, 1)
             old = jnp.where(position < valid, old * scale, NEG)
-            step = lax.broadcasted_iota(jnp.int32, new.shape, 0) // (QH // KVH)
+            step = lax.broadcasted_iota(jnp.int32, new.shape, 0) // group
             new = jnp.where(lax.broadcasted_iota(jnp.int32, new.shape, 1) <= step, new * scale, NEG)
             top = jnp.maximum(
                 jnp.max(old, axis=-1, keepdims=True), jnp.max(new, axis=-1, keepdims=True)
@@ -244,33 +262,30 @@
                 preferred_element_type=jnp.float32,
             ) + jnp.dot(
                 (new_weights / total).astype(jnp.bfloat16),
-                new_value_ref[0, head],
+                new_values,
                 preferred_element_type=jnp.float32,
             )
-            out_ref[0, head] = mixed.astype(jnp.bfloat16)
+            for k, (t, h) in enumerate(order):
+                out_ref[0, :, t * q_width + h * HD : t * q_width + (h + 1) * HD] = mixed[k : k + 1]
 
 
 def decode_here(length, active, fresh, cache_keys, cache_values, steps):
     rows, cache_len, kv_width = cache_keys.shape
-    heads = kv_width // HD
-    group = QH // KVH
-    q_width = heads * group * HD
-    fresh = fresh.reshape(rows, steps, q_width + 2 * kv_width)
-    queries = fresh[:, :, :q_width].reshape(rows, steps, heads, group, HD)
-    queries = queries.transpose(0, 2, 1, 3, 4).reshape(rows, heads, steps * group, HD)
-    new = fresh[:, :, q_width:].reshape(rows, steps, 2, heads, HD).transpose(2, 0, 3, 1, 4)
-    new = jnp.pad(new, ((0, 0), (0, 0), (0, 0), (0, 16 - steps), (0, 0)))
-    small = lambda n: pl.BlockSpec((1, heads, n, HD), lambda r, *_: (r, 0, 0, 0))
+    q_width = QH // KVH * kv_width
     cache = pl.BlockSpec((1, cache_len, kv_width), lambda r, *_: (r, 0, 0))
     out = pl.pallas_call(
         decode_kernel,
         grid_spec=pltpu.PrefetchScalarGridSpec(
             num_scalar_prefetch=2,
             grid=(rows,),
-            in_specs=[small(steps * group), small(16), small(16), cache, cache],
-            out_specs=small(steps * group),
-        ),
-        out_shape=jax.ShapeDtypeStruct((rows, heads, steps * group, HD), jnp.bfloat16),
+            in_specs=[
+                pl.BlockSpec((1, 1, fresh.shape[1]), lambda r, *_: (r, 0, 0)),
+                cache,
+                cache,
+            ],
+            out_specs=pl.BlockSpec((1, 1, steps * q_width), lambda r, *_: (r, 0, 0)),
+        ),
+        out_shape=jax.ShapeDtypeStruct((rows, 1, steps * q_width), jnp.float32),
         compiler_params=pltpu.CompilerParams(vmem_limit_bytes=16 * 2**20),
         cost_estimate=pl.CostEstimate(
             flops=4 * rows * cache_len * steps * q_width,
@@ -278,9 +293,8 @@
             transcendentals=0,
         ),
         name="decode_attention",
-    )(length, active, queries, new[0], new[1], cache_keys, cache_values)
-    out = out.reshape(rows, heads, steps, group, HD).transpose(0, 2, 1, 3, 4)
-    return out.reshape(rows, steps * q_width)
+    )(length, active, fresh[:, None], cache_keys, cache_values)
+    return out[:, 0].astype(jnp.bfloat16)
 
 
 def pick(mask, values):
@@ -352,9 +366,7 @@
         return jnp.where(inside, offset[:, None] + jnp.arange(resp_len)[None, :], -1)
 
     def starts(used, offset):
-        token = jnp.arange(full_cap, dtype=jnp.int32)
-        begun = (offset[None, :] <= token[:, None]) & (used[None, :] > 0)
-        return jnp.max(jnp.where(begun, offset[None, :], 0), axis=1)[:, None]
+        return jnp.where(used > 0, offset, 2 * full_cap)
 
     used_near, offset_near, total_near = layout(lengths, finished, own_shift, near)
     used_far, offset_far, total_far = layout(lengths, finished, own_shift, far)
@@ -396,21 +408,25 @@
         [lengths, finished, jnp.stack([most // resp_len, most % resp_len])]
     ).astype(jnp.bfloat16)
 
+    notes = jnp.pad(notes, (0, -notes.shape[0] % HD))[None]
+
     def noted(values):
-        block = jnp.pad(notes[None], ((0, 15), (0, values.shape[1] - notes.shape[0])))
-        return jnp.concatenate([values, block], axis=0)
+        line = jnp.pad(notes, ((0, 0), (0, values.shape[1] - notes.shape[1])))
+        return jnp.concatenate([values, line], axis=0)
 
     def read(values):
-        line = values[-16, : notes.shape[0]].astype(jnp.int32)
+        line = values[-1, : 2 * rows + 2].astype(jnp.int32)
         return line[:rows], line[rows : 2 * rows], line[2 * rows] * resp_len + line[2 * rows + 1]
 
     own_near = rank_mask(own_shift, own_rank, near)
     own_far = rank_mask(own_shift, own_rank, far)
     away_near, away_far = noted(pick(near_slot.T, fresh)), noted(pick(far_slot.T, fresh))
     back_near, back_far = along(away_near, -near), along(away_far, -far)
+    from_near, from_far, from_third = read(along(notes, near)), read(back_far), read(back_near)
     flat = ordered(flat, away_near, away_far)
     far_states = packed(place_far, 0, full_cap)
-    flat = ordered(flat, far_states)
+    far_first = far_states[: FAR_SHARES[0]]
+    flat = ordered(flat, far_first)
     near_states = packed(place_near, 0, full_cap)
     own_group = jnp.concatenate([own_near, own_far], axis=1)
     own_fresh = pick(own_group, jnp.concatenate([back_near[:cap], back_far[:cap]], axis=0))
@@ -440,12 +456,21 @@
     near_parts = [near_states[a:b] for a, b in zip(near_cuts, near_cuts[1:])]
     near_others = [across(piece) for piece in near_parts]
     far_parts = [far_states[a:b] for a, b in zip(far_cuts, far_cuts[1:])]
-    far_parts[0] = along(noted(far_parts[0]), far)
-    from_far = read(far_parts[0])
+    far_parts[0] = along(far_first, far)
     arrived_last = far_parts[0]
-    far_parts[0] = far_parts[0][:-16]
+    for came in (from_near, from_far, from_third):
+        most = jnp.maximum(most, came[2])
+    for k in range(1, reps):
+        pairs = [(i, (i + k) % reps) for i in range(reps)]
+        most = jnp.maximum(most, lax.ppermute(most, "rep", pairs))
+    used_a, offset_a, _ = arrived(from_near, near_shift, near)
     used_b, offset_b, _ = arrived(from_far, far_shift, far)
     start_far = starts(used_b, offset_b)
+    decoded = decode_here(
+        lengths, 1 - finished, own_fresh.astype(jnp.float32), cache_keys, cache_values, steps
+    )
+    came_near = along(pick(own_near.T, decoded), near)
+    came_far = along(pick(own_far.T, decoded), far)
     lows = near_cuts[:-1] + far_cuts[:-1]
     first_far, last = len(near_parts), len(lows) - 1
     owns = near_parts + far_parts
@@ -454,6 +479,8 @@
 
     def after_kernel(value, c):
         return ordered(value, sent[c]) if 0 <= c < len(sent) else value
+
+    last_sent = []
 
     def fetch(c):
         if first_far < c <= last:
@@ -476,11 +503,12 @@
         return both
 
     def finish(c):
-        got = after_kernel(turned[c], c + 3).astype(jnp.float32)
+        got = after_kernel(turned[c], c + 3)
+        if last_sent and first_far <= c < last:
+            got = ordered(got, last_sent[0])
+        got = got.astype(jnp.float32)
         both = kept[c][:, :width].astype(jnp.float32) + chips[c][:, :width].astype(jnp.float32)
         total = (both + got).astype(jnp.bfloat16)
-        if c == 0:
-            total = noted(total)
         done.append(along(total, near) if c < first_far else total)
         return total
 
@@ -488,7 +516,7 @@
     meet(0)
     tail = none
     for c, low in enumerate(lows):
-        before = [boths[0]] if c == 0 else [own_fresh] if c == 1 else []
+        before = [boths[0], decoded, most] if c == 0 else [came_near, came_far] if c == 1 else []
         fetch(c + 3 if c + 3 > first_far + 1 else -1)
         if c < last:
             meet(c + 1)
@@ -506,7 +534,7 @@
         send, keep, tail = layer(
             low,
             part,
-            row_start[low:high],
+            row_start,
             owns[c],
             others[c],
             cames[c],
@@ -517,27 +545,13 @@
         sent.append(send)
         kept.append(keep)
         crossed.append(beside(send))
-    for c in range(len(chips), last + 1):
-        gone = add(c)
+    for c in range(len(chips), last):
+        add(c)
+    while len(done) < first_far:
+        kept[last] = ordered(kept[last], finish(len(done)), done[0])
+    last_sent.append(add(last))
     for c in range(len(done), last + 1):
         finish(c)
-    decoded = decode_here(
-        ordered(lengths, gone),
-        1 - finished,
-        own_fresh,
-        cache_keys,
-        cache_values,
-        steps,
-    )
-    came_near = along(pick(own_near.T, decoded), near)
-    came_far = along(pick(own_far.T, decoded), far)
-    from_near, from_third = read(done[0]), read(back_near)
-    for came in (from_near, from_far, from_third):
-        most = jnp.maximum(most, came[2])
-    most = ordered(most, gone)
-    for k in range(1, reps):
-        pairs = [(i, (i + k) % reps) for i in range(reps)]
-        most = jnp.maximum(most, lax.ppermute(most, "rep", pairs))
     near_done, far_done = done[:first_far], done[first_far:]
 
     def overflow(near_x, far_x, near_kv, far_kv):
@@ -545,7 +559,7 @@
             other = across(own)
             came = beside(jnp.concatenate([own, other], axis=1))
             send, keep, _ = layer(
-                low, part, row_start[low:], own, other, came, kv, inverse_gain, weights
+                low, part, row_start, own, other, came, kv, inverse_gain, weights
             )
             chip = keep.astype(jnp.float32) + beside(send).astype(jnp.float32)
             got = across(chip[:, width:].astype(jnp.bfloat16))
@@ -571,7 +585,6 @@
         near_done, far_done = near_done + [near_more], far_done + [far_more]
         near_cuts, far_cuts = near_cuts + [full_cap], far_cuts + [full_cap]
     cuts = near_cuts[:-1] + [full_cap + cut_ for cut_ in far_cuts[:-1]]
-    used_a, offset_a, _ = arrived(from_near, near_shift, near)
     near_used, far_used = by_slot(near_hit, used_a), by_slot(far_hit, used_b)
     near_offset, far_offset = by_slot(near_hit, offset_a), by_slot(far_hit, offset_b)
     offset = near_offset + jnp.where(far_used > 0, far_offset + full_cap, 0)

time: 175 us -> 240 us (1.37); the launches traced: 172 us -> 240 us
  waiting for transfers between devices: 19.8 us -> 55.4 us
  Pallas kernels: 67 us -> 94.9 us
  starting transfers between devices: 31.8 us -> 37.5 us
  local copies, waits for them, and re-layouts: 16.5 us -> 11.6 us
  other arithmetic: 22.1 us -> 24.9 us
    ppermute x10 -> x14, waiting for transfers between devices: 0.03 us -> 37.4 us  [across(): return lax.ppermute(value, 'tp', [(i, i ^ 2) for i in range(tp)])]
    pallas_call x5 -> x7, Pallas kernels: 59.8 us -> 82.4 us  [layer(): pl.pallas_call(lambda *refs: layer_kernel(base, *refs), in_specs=[pl.Bloc...]
    pallas_call x1, Pallas kernels: 0.9 us -> 6.23 us  [decode_here(): pl.pallas_call(decode_kernel, grid_spec=pltpu.PrefetchScalarGridSpec(num_...]
    ppermute x10 -> x14, starting transfers between devices: 10.5 us -> 15.1 us  [across(): return lax.ppermute(value, 'tp', [(i, i ^ 2) for i in range(tp)])]
    slice x14 -> x4, local copies, waits for them, and re-layouts: 6.03 us -> 2.27 us  [the longest x1 1.11 us: two_shift_body(): far_states[capacity:]]
    ppermute x1, starting transfers between devices: 2.82 us -> 5.66 us  [two_shift_body(): most = jnp.maximum(most, lax.ppermute(most, 'rep', pairs))]
    ppermute x9 -> x12, starting transfers between devices: 16.4 us -> 13.9 us  [along(): lax.ppermute(value, 'inst', [(i, (i + shift) % count) for i in range(coun...]
    ppermute x9 -> x12, waiting for transfers between devices: 18.9 us -> 17.3 us  [along(): lax.ppermute(value, 'inst', [(i, (i + shift) % count) for i in range(coun...]
  transfers between devices with their start and end apart: 30 -> 41, of which waited for: 4 -> 8; matrix products, arithmetic and copies ran while one was open for 21% -> 16% of each run, Pallas kernels for 35% -> 37%
where the time goes in v1:
time: 240 us
  Pallas kernels  94.9 us (40%)
  waiting for transfers between devices  55.4 us (23%)
  starting transfers between devices  37.5 us (16%)
  other arithmetic  24.9 us (10%)
  local copies, waits for them, and re-layouts  11.6 us (5%)
  matrix products  7.93 us (3%)
  between operations  7.14 us (3%)
    pallas_call x7, Pallas kernels, layer(): pl.pallas_call(lambda *refs: layer_kernel(base, *refs), in_specs=[pl.Bloc...  82.4 us
    ppermute x14, waiting for transfers between devices, across(): return lax.ppermute(value, 'tp', [(i, i ^ 2) for i in range(tp)])  37.4 us
    ppermute x12, waiting for transfers between devices, along(): lax.ppermute(value, 'inst', [(i, (i + shift) % count) for i in range(coun...  17.3 us
    ppermute x14, starting transfers between devices, across(): return lax.ppermute(value, 'tp', [(i, i ^ 2) for i in range(tp)])  15.1 us
    ppermute x12, starting transfers between devices, along(): lax.ppermute(value, 'inst', [(i, (i + shift) % count) for i in range(coun...  13.9 us
    convert_element_type x5, other arithmetic, finish(): total = (both + got).astype(jnp.bfloat16)  6.98 us
    pallas_call x1, Pallas kernels, unpack(): pl.pallas_call(lambda *refs: unpack_kernel(cuts, *refs), grid_spec=pltpu....  6.25 us
    pallas_call x1, Pallas kernels, decode_here(): pl.pallas_call(decode_kernel, grid_spec=pltpu.PrefetchScalarGridSpec(num_...  6.23 us
  transfers between devices with their start and end apart: 41, of which 8 were waited for; matrix products, arithmetic and copies ran while one was open for 16% of the time, Pallas kernels for 37%

profile of v1, /device:TPU:0, one launch (start us, length us, event | category | flops | bytes accessed | tf_op | source)
XLA Modules:
  0.0 239.6 jit_solution(4512976899098484823)
XLA Ops:
  0.7 0.9 reshape.259
  1.6 1.4 fusion.52
  4.4 3.0 %collective-permute-start.14 = (bf16[1,128]{1,0:T(2,128)(2,1)S(1)}, bf16[1,128]{1,0:T(2,128)(2,1)S(1)}, u32[]{:S(2)}, u32[]{:S(2)}) collective-permute-start(bf16[1,128]{1,0:T(2,128)(2,1)S(1)} %fusion.38), channel_id=1, source_target_pairs={{0,4},{4,8},{8,12},{12,0},{1,5},{5,9},{9,13},{13,1},{2,6},{6,10},{... | collective-permute-start | bytes 776 | tf_op jit(solution)/shard_map/ppermute | solution.py:334
  7.5 0.9 pad_maximum_fusion.4
  9.6 1.3 broadcast_divide_fusion
  11.6 0.8 dynamic_slice.26
  12.5 0.7 select_reduce_fusion.4
  14.4 2.6 %collective-permute-start.11 = (bf16[8,3072]{1,0:T(8,128)(2,1)}, bf16[8,3072]{1,0:T(8,128)(2,1)}, u32[]{:S(2)}, u32[]{:S(2)}) collective-permute-start(bf16[8,3072]{1,0:T(8,128)(2,1)} %get-tuple-element.165), channel_id=1, source_target_pairs={{0,8},{4,12},{8,0},{12,4},{1,9},{5,13},{9,1},{13,5},{2,10},{6,14},... | collective-permute-start | bytes 147464 | tf_op jit(solution)/shard_map/ppermute | solution.py:334
  17.0 1.3 collective-permute-start.10
  18.4 2.9 %multiply_convert_fusion.1 = bf16[896,768]{1,0:T(8,128)(2,1)S(1)} fusion(bf16[1792,768]{1,0:T(8,128)(2,1)S(1)} %bitcast.57, s32[1792]{0:T(1024)S(1)} %get-tuple-element.171, f32[768]{0:T(1024)S(1)} %dynamic_slice.26), kind=kOutput, calls=%fused_computation.21 | convolution fusion | flops 2469232640 | bytes 4139008 | tf_op jit(solution)/shard_map/dot_general | solution.py:381
  21.3 1.0 fusion.54
  22.3 2.9 %multiply_convert_fusion = bf16[896,768]{1,0:T(8,128)(2,1)S(1)} fusion(bf16[1792,768]{1,0:T(8,128)(2,1)S(1)} %bitcast.56, s32[1792]{0:T(1024)S(1)} %get-tuple-element.172, f32[768]{0:T(1024)S(1)} %dynamic_slice.26), kind=kOutput, calls=%fused_computation.20 | convolution fusion | flops 2469232640 | bytes 4139008 | tf_op jit(solution)/shard_map/dot_general | solution.py:381
  25.2 0.7 fusion.57
  26.3 0.8 slice.210
  27.0 1.7 collective-permute-start.15
  30.4 1.0 fusion.4
  31.6 1.5 copy-done.3
  33.1 6.2 %decode_attention.1 = f32[14,1,2048]{2,1,0:T(1,128)S(1)} custom-call(s32[14]{0:T(128)S(1)} %copy-done.4, s32[14]{0:T(128)S(1)} %get-tuple-element.168.active_ref, f32[14,1,3072]{2,1,0:T(1,128)S(1)} %reshape.263.fresh_ref, bf16[14,256,256]{2,1,0:T(8,128)(2,1)S(1)} %copy-done.2, bf16[14,256,256]{2,1,0:T(8,128)(2,1)S(1)} %copy-done.3), custom_call_target="tpu_custom_call" | custom-call | flops 29360128 | bytes 7340032 | tf_op jit(solution)/shard_map/decode_attention/pallas_call | solution.py:276
  41.3 2.1 pad_maximum_fusion.3
  47.3 5.7 %collective-permute-start.17 = (s32[]{:T(128)}, s32[]{:T(128)}, u32[]{:S(2)}, u32[]{:S(2)}) collective-permute-start(s32[]{:T(128)} %max.18), channel_id=1, source_target_pairs={{0,16},{16,0},{1,17},{17,1},{2,18},{18,2},{3,19},{19,3},{4,20},{20... | collective-permute-start | bytes 20 | tf_op jit(solution)/shard_map/ppermute | solution.py:465
  53.0 0.7 select_reduce_fusion.2
  54.7 1.1 collective-permute-start.24
  55.8 1.5 collective-permute-start.22
  57.6 16.8 %prefill_layer.9 = (bf16[320,1536]{1,0:T(8,128)(2,1)S(1)}, bf16[320,1536]{1,0:T(8,128)(2,1)S(1)}, bf16[128,512]{1,0:T(8,128)(2,1)S(1)}) custom-call(s32[1]{0:T(128)} %bitcast.13.refs_0_, s32[14]{0:T(128)S(1)} %copy-done.29, bf16[320,768]{1,0:T(8,128)(2,1)S(1)} %slice.206.refs_2_, bf16[320,768]{1,0:T(8,128)(2,1)} %collective-permute-done.15.refs_3_, ...), custom_call_target="tpu_custom_call" | custom-call | flops 15099494400 | bytes 1024 | tf_op jit(solution)/shard_map/prefill_layer/pallas_call | solution.py:152
  74.9 1.0 constant_dynamic-update-slice_fusion.1
  76.1 0.9 collective-permute-start.25
  76.9 1.6 collective-permute-start.28
  78.6 14.4 %prefill_layer.10 = (bf16[384,1536]{1,0:T(8,128)(2,1)S(1)}, bf16[384,1536]{1,0:T(8,128)(2,1)S(1)}, bf16[128,512]{1,0:T(8,128)(2,1)}) custom-call(s32[1]{0:T(128)} %bitcast.13.refs_0_, s32[14]{0:T(128)S(1)} %copy-done.29, bf16[384,768]{1,0:T(8,128)(2,1)S(1)} %slice.208.refs_2_, bf16[384,768]{1,0:T(8,128)(2,1)S(1)} %collective-permute-done.18.refs_3_, ...), custom_call_target="tpu_custom_call" | custom-call | flops 18119393280 | bytes 1024 | tf_op jit(solution)/shard_map/prefill_layer/pallas_call | solution.py:152
  93.1 1.6 collective-permute-start.29
  95.7 10.3 %prefill_layer.11 = (bf16[256,1536]{1,0:T(8,128)(2,1)S(1)}, bf16[256,1536]{1,0:T(8,128)(2,1)S(1)}, bf16[128,512]{1,0:T(8,128)(2,1)S(1)}) custom-call(s32[1]{0:T(128)} %bitcast.13.refs_0_, s32[14]{0:T(128)S(1)} %compare_select_fusion.refs_1_, bf16[256,768]{1,0:T(8,128)(2,1)} %collective-permute-done.21.refs_2_, ...), custom_call_target="tpu_custom_call" | custom-call | flops 12079595520 | bytes 1024 | tf_op jit(solution)/shard_map/prefill_layer/pallas_call | solution.py:152
  106.7 1.1 add_convert_fusion.1
  107.8 1.5 collective-permute-start.32
  109.3 10.9 %prefill_layer.12 = (bf16[256,1536]{1,0:T(8,128)(2,1)}, bf16[256,1536]{1,0:T(8,128)(2,1)S(1)}, bf16[128,512]{1,0:T(8,128)(2,1)S(1)}) custom-call(s32[1]{0:T(128)} %bitcast.13.refs_0_, s32[14]{0:T(128)S(1)} %copy-done.32, bf16[256,768]{1,0:T(8,128)(2,1)S(1)} %collective-permute-done.24.refs_2_, bf16[256,768]{1,0:T(8,128)(2,1)S(1)} %collective-permute-done.25.refs_3_, ...), custom_call_target="tpu_custom_call" | custom-call | flops 12079595520 | bytes 1024 | tf_op jit(solution)/shard_map/prefill_layer/pallas_call | solution.py:152
  120.2 1.0 add_convert_fusion.2
  121.2 1.5 collective-permute-start.31
  122.8 1.0 add_convert_fusion.7
  123.7 8.8 %prefill_layer.13 = (bf16[192,1536]{1,0:T(8,128)(2,1)}, bf16[192,1536]{1,0:T(8,128)(2,1)S(1)}, bf16[128,512]{1,0:T(8,128)(2,1)}) custom-call(s32[1]{0:T(128)} %bitcast.13.refs_0_, s32[14]{0:T(128)S(1)} %copy-done.32, bf16[192,768]{1,0:T(8,128)(2,1)S(1)} %collective-permute-done.28.refs_2_, bf16[192,768]{1,0:T(8,128)(2,1)S(1)} %collective-permute-done.29.refs_3_, ...), custom_call_target="tpu_custom_call" | custom-call | flops 9059696640 | bytes 1024 | tf_op jit(solution)/shard_map/prefill_layer/pallas_call | solution.py:152
  132.8 1.1 collective-permute-start.36
  133.9 2.3 add_convert_fusion
  136.2 1.1 collective-permute-done.31.refs_2_
  137.3 1.9 add_convert_fusion.5
  139.7 1.8 add_convert_fusion.9
  141.4 1.5 collective-permute-start.40
  143.8 73.9 %conditional.1 = (bf16[192,768]{1,0:T(8,128)(2,1)}, bf16[192,768]{1,0:T(8,128)(2,1)S(1)}) conditional(s32[]{:T(128)} %convert_element_type.233, () %tuple.66, (s32[]{:T(128)}, bf16[896,768]{1,0:T(8,128)(2,1)}, s32[14]{0:T(128)S(1)}, bf16[128,512]{1,0:T(8,128)(2,1)}, f32[1,3072]{1,0:T(1,128)S(1)}, /*index=5*/bf16[3072,1024]{1,0:T(8,128)(2,1)}, ...), branch_computations={%region_15.16_spmd, %region_16.17_spmd} | conditional | flops 18124406784 | bytes 79694448 | solution.py:576
  143.8 1.1 slice.108.refs_2_
  145.5 1.1 slice.111
  146.6 2.3 collective-permute-start.5
  148.9 16.5 %collective-permute-done.refs_3_ = bf16[192,768]{1,0:T(8,128)(2,1)S(1)} collective-permute-done((bf16[192,768]{1,0:T(8,128)(2,1)S(1)}, bf16[192,768]{1,0:T(8,128)(2,1)S(1)}, u32[]{:S(2)}, u32[]{:S(2)}) %collective-permute-start) | collective-permute-done | bytes 294944 | tf_op jit(solution)/shard_map/cond/branch_1_fun/ppermute | solution.py:337
  165.6 1.1 collective-permute-start.6
  166.7 8.3 %collective-permute-done.6.refs_3_ = bf16[192,768]{1,0:T(8,128)(2,1)S(1)} collective-permute-done((bf16[192,768]{1,0:T(8,128)(2,1)S(1)}, bf16[192,768]{1,0:T(8,128)(2,1)S(1)}, u32[]{:S(2)}, u32[]{:S(2)}) %collective-permute-start.6) | collective-permute-done | bytes 294944 | tf_op jit(solution)/shard_map/cond/branch_1_fun/ppermute | solution.py:337
  175.2 12.7 %prefill_layer.7 = (bf16[192,1536]{1,0:T(8,128)(2,1)S(1)}, bf16[192,1536]{1,0:T(8,128)(2,1)S(1)}, bf16[128,512]{1,0:T(8,128)(2,1)}) custom-call(s32[1]{0:T(128)} %bitcast.refs_0_, s32[14]{0:T(128)S(1)} %get-tuple-element.27.refs_1_, bf16[192,768]{1,0:T(8,128)(2,1)S(1)} %slice.108.refs_2_, bf16[192,768]{1,0:T(8,128)(2,1)S(1)} %collective-permute-done.refs_3_, ...), custom_call_target="tpu_custom_call" | custom-call | flops 9059696640 | bytes 1024 | tf_op jit(solution)/shard_map/cond/branch_1_fun/prefill_layer/pallas_call | solution.py:152
  187.9 0.8 collective-permute-start.2
  188.8 8.5 %prefill_layer.8 = (bf16[192,1536]{1,0:T(8,128)(2,1)S(1)}, bf16[192,1536]{1,0:T(8,128)(2,1)S(1)}, bf16[128,512]{1,0:T(8,128)(2,1)}) custom-call(s32[1]{0:T(128)} %bitcast.refs_0_, s32[14]{0:T(128)S(1)} %get-tuple-element.37.refs_1_, bf16[192,768]{1,0:T(8,128)(2,1)S(1)} %collective-permute-done.5.refs_2_, ...), custom_call_target="tpu_custom_call" | custom-call | flops 9059696640 | bytes 1024 | tf_op jit(solution)/shard_map/cond/branch_1_fun/prefill_layer/pallas_call | solution.py:152
  197.5 1.1 collective-permute-start.3
  198.6 0.7 collective-permute-done.8
  199.5 1.1 collective-permute-start.9
  200.6 6.8 %collective-permute-done.3 = bf16[192,768]{1,0:T(8,128)(2,1)S(1)} collective-permute-done((bf16[192,768]{1,0:T(8,128)(2,1)S(1)}, bf16[192,768]{1,0:T(8,128)(2,1)S(1)}, u32[]{:S(2)}, u32[]{:S(2)}) %collective-permute-start.3) | collective-permute-done | bytes 294944 | tf_op jit(solution)/shard_map/cond/branch_1_fun/ppermute | solution.py:337
  207.6 5.8 %collective-permute-done.9 = bf16[192,768]{1,0:T(8,128)(2,1)S(1)} collective-permute-done((bf16[192,768]{1,0:T(8,128)(2,1)S(1)}, bf16[192,768]{1,0:T(8,128)(2,1)S(1)}, u32[]{:S(2)}, u32[]{:S(2)}) %collective-permute-start.9) | collective-permute-done | bytes 294944 | tf_op jit(solution)/shard_map/cond/branch_1_fun/ppermute | solution.py:337
  213.4 4.3 %collective-permute-done.4 = bf16[192,768]{1,0:T(8,128)(2,1)} collective-permute-done((bf16[192,768]{1,0:T(8,128)(2,1)S(1)}, bf16[192,768]{1,0:T(8,128)(2,1)}, u32[]{:S(2)}, u32[]{:S(2)}) %collective-permute-start.4) | collective-permute-done | bytes 294944 | tf_op jit(solution)/shard_map/cond/branch_1_fun/ppermute | solution.py:334
  217.7 1.3 add_convert_fusion.6.refs_5_
  219.0 1.2 add_convert_fusion.8.refs_7_
  220.1 1.3 add_convert_fusion.4.refs_6_
  221.4 11.9 %collective-permute-done.35.refs_3_ = bf16[384,768]{1,0:T(8,128)(2,1)S(1)} collective-permute-done((bf16[384,768]{1,0:T(8,128)(2,1)}, bf16[384,768]{1,0:T(8,128)(2,1)S(1)}, u32[]{:S(2)}, u32[]{:S(2)}) %collective-permute-start.35) | collective-permute-done | bytes 589856 | tf_op jit(solution)/shard_map/ppermute | solution.py:334
  233.3 6.3 %unpack_slots.1 = bf16[14,128,768]{2,1,0:T(8,128)(2,1)} custom-call(s32[14]{0:T(128)S(1)} %get-tuple-element.161.refs_0_, s32[14]{0:T(128)S(1)} %get-tuple-element.160.refs_1_, bf16[320,768]{1,0:T(8,128)(2,1)} %collective-permute-done.31.refs_2_, bf16[384,768]{1,0:T(8,128)(2,1)S(1)} %collective-permute-done.35.refs_3_, ...), custom_call_target="tpu_custom_call" | custom-call | tf_op jit(solution)/shard_map/unpack_slots/pallas_call | solution.py:200
  (202 shorter events, 13.6 us)
Async XLA Ops:
  0.6 17.7 %copy-start = (bf16[14,128,768]{2,1,0:T(8,128)(2,1)S(1)}, bf16[14,128,768]{2,1,0:T(8,128)(2,1)}, u32[]{:S(2)}) copy-start(bf16[14,128,768]{2,1,0:T(8,128)(2,1)} %param.21) | copy-start | bytes 8257540
  1.6 19.6 %copy-start.21 = (pred[14]{0:T(512)(128)(4,1)}, pred[14]{0:T(512)(128)(4,1)S(1)}, u32[]{:S(2)}) copy-start(pred[14]{0:T(512)(128)(4,1)S(1)} %get-tuple-element.150) | copy-start | bytes 46
  4.4 7.9 %collective-permute-start.14 = (bf16[1,128]{1,0:T(2,128)(2,1)S(1)}, bf16[1,128]{1,0:T(2,128)(2,1)S(1)}, u32[]{:S(2)}, u32[]{:S(2)}) collective-permute-start(bf16[1,128]{1,0:T(2,128)(2,1)S(1)} %fusion.38), channel_id=1, source_target_pairs={{0,4},{4,8},{8,12},{12,0},{1,5},{5,9},{9,13},{13,1},{2,6},{6,10},{... | collective-permute-start | bytes 776 | tf_op jit(solution)/shard_map/ppermute | solution.py:334
  7.5 13.8 %copy-start.23 = (pred[14]{0:T(512)(128)(4,1)}, pred[14]{0:T(512)(128)(4,1)S(1)}, u32[]{:S(2)}) copy-start(pred[14]{0:T(512)(128)(4,1)S(1)} %broadcast_compare_fusion) | copy-start | bytes 46
  14.4 16.0 %collective-permute-start.11 = (bf16[8,3072]{1,0:T(8,128)(2,1)}, bf16[8,3072]{1,0:T(8,128)(2,1)}, u32[]{:S(2)}, u32[]{:S(2)}) collective-permute-start(bf16[8,3072]{1,0:T(8,128)(2,1)} %get-tuple-element.165), channel_id=1, source_target_pairs={{0,8},{4,12},{8,0},{12,4},{1,9},{5,13},{9,1},{13,5},{2,10},{6,14},... | collective-permute-start | bytes 147464 | tf_op jit(solution)/shard_map/ppermute | solution.py:334
  17.0 13.4 %collective-permute-start.10 = (bf16[8,3072]{1,0:T(8,128)(2,1)}, bf16[8,3072]{1,0:T(8,128)(2,1)}, u32[]{:S(2)}, u32[]{:S(2)}) collective-permute-start(bf16[8,3072]{1,0:T(8,128)(2,1)} %get-tuple-element.164), channel_id=1, source_target_pairs={{0,12},{4,0},{8,4},{12,8},{1,13},{5,1},{9,5},{13,9},{2,14},{6,2},{... | collective-permute-start | bytes 147464 | tf_op jit(solution)/shard_map/ppermute | solution.py:334
  26.0 28.6 %collective-permute-start.21 = (bf16[256,768]{1,0:T(8,128)(2,1)}, bf16[256,768]{1,0:T(8,128)(2,1)}, u32[]{:S(2)}, u32[]{:S(2)}) collective-permute-start(bf16[256,768]{1,0:T(8,128)(2,1)} %get-tuple-element.147), channel_id=1, source_target_pairs={{0,8},{4,12},{8,0},{12,4},{1,9},{5,13},{9,1},{13,5},{2,10},{6,14},... | collective-permute-start | bytes 1179656 | tf_op jit(solution)/shard_map/ppermute | solution.py:334
  27.0 14.3 %collective-permute-start.15 = (bf16[320,768]{1,0:T(8,128)(2,1)S(1)}, bf16[320,768]{1,0:T(8,128)(2,1)}, u32[]{:S(2)}, u32[]{:S(2)}) collective-permute-start(bf16[320,768]{1,0:T(8,128)(2,1)S(1)} %slice.206.refs_2_), channel_id=1, source_target_pairs={{0,2},{1,3},{2,0},{3,1},{4,6},{5,7},{6,4},{7,5},{8,10},{9,11},{10,... | collective-permute-start | bytes 1474568 | tf_op jit(solution)/shard_map/ppermute | solution.py:337
  30.0 25.8 %collective-permute-start.18 = (bf16[384,768]{1,0:T(8,128)(2,1)S(1)}, bf16[384,768]{1,0:T(8,128)(2,1)S(1)}, u32[]{:S(2)}, u32[]{:S(2)}) collective-permute-start(bf16[384,768]{1,0:T(8,128)(2,1)S(1)} %slice.208.refs_2_), channel_id=1, source_target_pairs={{0,2},{1,3},{2,0},{3,1},{4,6},{5,7},{6,4},{7,5},{8,10},{9,11},{10,... | collective-permute-start | bytes 1769480 | tf_op jit(solution)/shard_map/ppermute | solution.py:337
  39.3 14.4 %copy-start.20 = (s32[14]{0:T(128)S(1)}, s32[14]{0:T(128)}, u32[]{:S(2)}) copy-start(s32[14]{0:T(128)} %copy-done.18) | copy-start | bytes 172
  39.3 14.4 %copy-start.22 = (pred[14]{0:T(512)(128)(4,1)S(1)}, pred[14]{0:T(512)(128)(4,1)}, u32[]{:S(2)}) copy-start(pred[14]{0:T(512)(128)(4,1)} %copy-done.21) | copy-start | bytes 46
  39.4 15.3 %copy-start.9 = (bf16[256,768]{1,0:T(8,128)(2,1)S(1)}, bf16[256,768]{1,0:T(8,128)(2,1)}, u32[]{:S(2)}) copy-start(bf16[256,768]{1,0:T(8,128)(2,1)} %get-tuple-element.99) | copy-start | bytes 1179652
  39.8 36.2 %collective-permute-start.13 = (bf16[7,2048]{1,0:T(8,128)(2,1)S(1)}, bf16[7,2048]{1,0:T(8,128)(2,1)S(1)}, u32[]{:S(2)}, u32[]{:S(2)}) collective-permute-start(bf16[7,2048]{1,0:T(8,128)(2,1)S(1)} %convolution_convert_fusion.4), channel_id=1, source_target_pairs={{0,8},{4,12},{8,0},{12,4},{1,9},{5,13},{9,1},{13,5},{2,10},{6,14},... | collective-permute-start | bytes 86024 | tf_op jit(solution)/shard_map/ppermute | solution.py:334
  43.4 14.1 %copy-start.13 = (f32[3072]{0:T(1024)S(1)}, f32[3072]{0:T(1024)}, u32[]{:S(2)}) copy-start(f32[3072]{0:T(1024)} %broadcast_divide_fusion) | copy-start | bytes 36868
  43.4 14.1 %copy-start.29 = (s32[14]{0:T(128)S(1)}, s32[14]{0:T(128)}, u32[]{:S(2)}) copy-start(s32[14]{0:T(128)} %compare_select_fusion.1.refs_1_) | copy-start | bytes 172
  43.4 14.0 %collective-permute-start.16 = (bf16[320,1536]{1,0:T(8,128)(2,1)}, bf16[320,1536]{1,0:T(8,128)(2,1)S(1)}, u32[]{:S(2)}, u32[]{:S(2)}) collective-permute-start(bf16[320,1536]{1,0:T(8,128)(2,1)} %pad_maximum_fusion.3), channel_id=1, source_target_pairs={{0,1},{1,0},{2,3},{3,2},{4,5},{5,4},{6,7},{7,6},{8,9},{9,8},{10,11... | collective-permute-start | bytes 2949128 | tf_op jit(solution)/shard_map/ppermute | solution.py:340
  47.3 6.6 %collective-permute-start.17 = (s32[]{:T(128)}, s32[]{:T(128)}, u32[]{:S(2)}, u32[]{:S(2)}) collective-permute-start(s32[]{:T(128)} %max.18), channel_id=1, source_target_pairs={{0,16},{16,0},{1,17},{17,1},{2,18},{18,2},{3,19},{19,3},{4,20},{20... | collective-permute-start | bytes 20 | tf_op jit(solution)/shard_map/ppermute | solution.py:465
  53.0 42.7 %copy-start.31 = (s32[14]{0:T(128)}, s32[14]{0:T(128)S(1)}, u32[]{:S(2)}) copy-start(s32[14]{0:T(128)S(1)} %compare_select_fusion.refs_1_) | copy-start | bytes 172
  54.0 22.1 %collective-permute-start.12 = (bf16[7,2048]{1,0:T(8,128)(2,1)S(1)}, bf16[7,2048]{1,0:T(8,128)(2,1)S(1)}, u32[]{:S(2)}, u32[]{:S(2)}) collective-permute-start(bf16[7,2048]{1,0:T(8,128)(2,1)S(1)} %convolution_convert_fusion.5), channel_id=1, source_target_pairs={{0,4},{4,8},{8,12},{12,0},{1,5},{5,9},{9,13},{13,1},{2,6},{6,10},{... | collective-permute-start | bytes 86024 | tf_op jit(solution)/shard_map/ppermute | solution.py:334
  54.7 21.4 %collective-permute-start.24 = (bf16[256,768]{1,0:T(8,128)(2,1)S(1)}, bf16[256,768]{1,0:T(8,128)(2,1)S(1)}, u32[]{:S(2)}, u32[]{:S(2)}) collective-permute-start(bf16[256,768]{1,0:T(8,128)(2,1)S(1)} %copy-done.9), channel_id=1, source_target_pairs={{0,8},{4,12},{8,0},{12,4},{1,9},{5,13},{9,1},{13,5},{2,10},{6,14},... | collective-permute-start | bytes 1179656 | tf_op jit(solution)/shard_map/ppermute | solution.py:334
  55.8 18.6 %collective-permute-start.22 = (bf16[256,768]{1,0:T(8,128)(2,1)}, bf16[256,768]{1,0:T(8,128)(2,1)S(1)}, u32[]{:S(2)}, u32[]{:S(2)}) collective-permute-start(bf16[256,768]{1,0:T(8,128)(2,1)} %collective-permute-done.21.refs_2_), channel_id=1, source_target_pairs={{0,2},{1,3},{2,0},{3,1},{4,6},{5,7},{6,4},{7,5},{8,10},{9,11},{10,... | collective-permute-start | bytes 1179656 | tf_op jit(solution)/shard_map/ppermute | solution.py:337
  57.4 21.2 %collective-permute-start.20 = (bf16[384,1536]{1,0:T(8,128)(2,1)S(1)}, bf16[384,1536]{1,0:T(8,128)(2,1)S(1)}, u32[]{:S(2)}, u32[]{:S(2)}) collective-permute-start(bf16[384,1536]{1,0:T(8,128)(2,1)S(1)} %pad_maximum_fusion.2), channel_id=1, source_target_pairs={{0,1},{1,0},{2,3},{3,2},{4,5},{5,4},{6,7},{7,6},{8,9},{9,8},{10,11... | collective-permute-start | bytes 3538952 | tf_op jit(solution)/shard_map/ppermute | solution.py:340
  57.5 21.1 %slice-start = ((s8[6291456]{0:T(1024)(128)(4,1)}), s8[4194304]{0:T(1024)(128)(4,1)S(1)}, s32[]{:S(2)}) async-start(s8[6291456]{0:T(1024)(128)(4,1)} %bitcast.69), calls=%async_computation | async-start | bytes 8388608
  57.5 21.1 %slice-start.4 = ((s8[6291456]{0:T(1024)(128)(4,1)}), s8[4194304]{0:T(1024)(128)(4,1)S(1)}, s32[]{:S(2)}) async-start(s8[6291456]{0:T(1024)(128)(4,1)} %bitcast.73), calls=%async_computation.4 | async-start | bytes 8388608
  57.5 21.1 %slice-start.1 = ((s8[6291456]{0:T(1024)(128)(4,1)}), s8[2097152]{0:T(1024)(128)(4,1)S(1)}, s32[]{:S(2)}) async-start(s8[6291456]{0:T(1024)(128)(4,1)} %bitcast.69), calls=%async_computation.1 | async-start | bytes 4194304
  57.5 21.1 %slice-start.5 = ((s8[6291456]{0:T(1024)(128)(4,1)}), s8[2097152]{0:T(1024)(128)(4,1)S(1)}, s32[]{:S(2)}) async-start(s8[6291456]{0:T(1024)(128)(4,1)} %bitcast.73), calls=%async_computation.5 | async-start | bytes 4194304
  57.6 21.1 %copy-start.27 = (bf16[3072,256]{1,0:T(8,128)(2,1)S(1)}, bf16[3072,256]{1,0:T(8,128)(2,1)}, u32[]{:S(2)}) copy-start(bf16[3072,256]{1,0:T(8,128)(2,1)} %refs_9_.9) | copy-start | bytes 4718596
  74.4 20.6 %collective-permute-start.19 = (bf16[320,1536]{1,0:T(8,128)(2,1)S(1)}, bf16[320,1536]{1,0:T(8,128)(2,1)S(1)}, u32[]{:S(2)}, u32[]{:S(2)}) collective-permute-start(bf16[320,1536]{1,0:T(8,128)(2,1)S(1)} %get-tuple-element.92), channel_id=1, source_target_pairs={{0,1},{1,0},{2,3},{3,2},{4,5},{5,4},{6,7},{7,6},{8,9},{9,8},{10,11... | collective-permute-start | bytes 2949128 | tf_op jit(solution)/shard_map/ppermute | solution.py:340
  76.0 19.7 %collective-permute-start.27 = (bf16[256,1536]{1,0:T(8,128)(2,1)S(1)}, bf16[256,1536]{1,0:T(8,128)(2,1)S(1)}, u32[]{:S(2)}, u32[]{:S(2)}) collective-permute-start(bf16[256,1536]{1,0:T(8,128)(2,1)S(1)} %constant_dynamic-update-slice_fusion), channel_id=1, source_target_pairs={{0,1},{1,0},{2,3},{3,2},{4,5},{5,4},{6,7},{7,6},{8,9},{9,8},{10,11... | collective-permute-start | bytes 2359304 | tf_op jit(solution)/shard_map/ppermute | solution.py:340
  76.1 17.0 %copy-start.11 = (bf16[7,2048]{1,0:T(8,128)(2,1)}, bf16[7,2048]{1,0:T(8,128)(2,1)S(1)}, u32[]{:S(2)}) copy-start(bf16[7,2048]{1,0:T(8,128)(2,1)S(1)} %collective-permute-done.12) | copy-start | bytes 86020
  76.1 18.6 %collective-permute-start.25 = (bf16[256,768]{1,0:T(8,128)(2,1)S(1)}, bf16[256,768]{1,0:T(8,128)(2,1)S(1)}, u32[]{:S(2)}, u32[]{:S(2)}) collective-permute-start(bf16[256,768]{1,0:T(8,128)(2,1)S(1)} %collective-permute-done.24.refs_2_), channel_id=1, source_target_pairs={{0,2},{1,3},{2,0},{3,1},{4,6},{5,7},{6,4},{7,5},{8,10},{9,11},{10,... | collective-permute-start | bytes 1179656 | tf_op jit(solution)/shard_map/ppermute | solution.py:337
  76.9 16.1 %collective-permute-start.28 = (bf16[192,768]{1,0:T(8,128)(2,1)S(1)}, bf16[192,768]{1,0:T(8,128)(2,1)S(1)}, u32[]{:S(2)}, u32[]{:S(2)}) collective-permute-start(bf16[192,768]{1,0:T(8,128)(2,1)S(1)} %copy-done.10), channel_id=1, source_target_pairs={{0,8},{4,12},{8,0},{12,4},{1,9},{5,13},{9,1},{13,5},{2,10},{6,14},... | collective-permute-start | bytes 884744 | tf_op jit(solution)/shard_map/ppermute | solution.py:334
  93.1 13.6 %collective-permute-start.30 = (bf16[384,1536]{1,0:T(8,128)(2,1)S(1)}, bf16[384,1536]{1,0:T(8,128)(2,1)S(1)}, u32[]{:S(2)}, u32[]{:S(2)}) collective-permute-start(bf16[384,1536]{1,0:T(8,128)(2,1)S(1)} %get-tuple-element.97), channel_id=1, source_target_pairs={{0,1},{1,0},{2,3},{3,2},{4,5},{5,4},{6,7},{7,6},{8,9},{9,8},{10,11... | collective-permute-start | bytes 3538952 | tf_op jit(solution)/shard_map/ppermute | solution.py:340
  93.1 13.0 %collective-permute-start.29 = (bf16[192,768]{1,0:T(8,128)(2,1)S(1)}, bf16[192,768]{1,0:T(8,128)(2,1)S(1)}, u32[]{:S(2)}, u32[]{:S(2)}) collective-permute-start(bf16[192,768]{1,0:T(8,128)(2,1)S(1)} %collective-permute-done.28.refs_2_), channel_id=1, source_target_pairs={{0,2},{1,3},{2,0},{3,1},{4,6},{5,7},{6,4},{7,5},{8,10},{9,11},{10,... | collective-permute-start | bytes 884744 | tf_op jit(solution)/shard_map/ppermute | solution.py:337
  94.7 14.5 %collective-permute-start.26 = (bf16[256,1536]{1,0:T(8,128)(2,1)S(1)}, bf16[256,1536]{1,0:T(8,128)(2,1)S(1)}, u32[]{:S(2)}, u32[]{:S(2)}) collective-permute-start(bf16[256,1536]{1,0:T(8,128)(2,1)S(1)} %constant_dynamic-update-slice_fusion.2), channel_id=1, source_target_pairs={{0,1},{1,0},{2,3},{3,2},{4,5},{5,4},{6,7},{7,6},{8,9},{9,8},{10,11... | collective-permute-start | bytes 2359304 | tf_op jit(solution)/shard_map/ppermute | solution.py:340
  95.1 25.1 %collective-permute-start.23 = (bf16[320,768]{1,0:T(8,128)(2,1)S(1)}, bf16[320,768]{1,0:T(8,128)(2,1)S(1)}, u32[]{:S(2)}, u32[]{:S(2)}) collective-permute-start(bf16[320,768]{1,0:T(8,128)(2,1)S(1)} %add_convert_fusion.3), channel_id=1, source_target_pairs={{0,2},{1,3},{2,0},{3,1},{4,6},{5,7},{6,4},{7,5},{8,10},{9,11},{10,... | collective-permute-start | bytes 1474568 | tf_op jit(solution)/shard_map/ppermute | solution.py:337
  106.0 16.8 %collective-permute-start.34 = (bf16[256,1536]{1,0:T(8,128)(2,1)S(1)}, bf16[256,1536]{1,0:T(8,128)(2,1)S(1)}, u32[]{:S(2)}, u32[]{:S(2)}) collective-permute-start(bf16[256,1536]{1,0:T(8,128)(2,1)S(1)} %get-tuple-element.108), channel_id=1, source_target_pairs={{0,1},{1,0},{2,3},{3,2},{4,5},{5,4},{6,7},{7,6},{8,9},{9,8},{10,11... | collective-permute-start | bytes 2359304 | tf_op jit(solution)/shard_map/ppermute | solution.py:340
  106.1 17.6 %collective-permute-start.33 = (bf16[192,1536]{1,0:T(8,128)(2,1)S(1)}, bf16[192,1536]{1,0:T(8,128)(2,1)S(1)}, u32[]{:S(2)}, u32[]{:S(2)}) collective-permute-start(bf16[192,1536]{1,0:T(8,128)(2,1)S(1)} %constant_dynamic-update-slice_fusion.4), channel_id=1, source_target_pairs={{0,1},{1,0},{2,3},{3,2},{4,5},{5,4},{6,7},{7,6},{8,9},{9,8},{10,11... | collective-permute-start | bytes 1769480 | tf_op jit(solution)/shard_map/ppermute | solution.py:340
  107.8 26.1 %collective-permute-start.32 = (bf16[384,768]{1,0:T(8,128)(2,1)}, bf16[384,768]{1,0:T(8,128)(2,1)}, u32[]{:S(2)}, u32[]{:S(2)}) collective-permute-start(bf16[384,768]{1,0:T(8,128)(2,1)} %add_convert_fusion.1), channel_id=1, source_target_pairs={{0,2},{1,3},{2,0},{3,1},{4,6},{5,7},{6,4},{7,5},{8,10},{9,11},{10,... | collective-permute-start | bytes 1769480 | tf_op jit(solution)/shard_map/ppermute | solution.py:337
  120.2 17.0 %collective-permute-start.38 = (bf16[256,1536]{1,0:T(8,128)(2,1)}, bf16[256,1536]{1,0:T(8,128)(2,1)}, u32[]{:S(2)}, u32[]{:S(2)}) collective-permute-start(bf16[256,1536]{1,0:T(8,128)(2,1)} %get-tuple-element.115), channel_id=1, source_target_pairs={{0,1},{1,0},{2,3},{3,2},{4,5},{5,4},{6,7},{7,6},{8,9},{9,8},{10,11... | collective-permute-start | bytes 2359304 | tf_op jit(solution)/shard_map/ppermute | solution.py:340
  121.2 16.0 %collective-permute-start.31 = (bf16[320,768]{1,0:T(8,128)(2,1)}, bf16[320,768]{1,0:T(8,128)(2,1)}, u32[]{:S(2)}, u32[]{:S(2)}) collective-permute-start(bf16[320,768]{1,0:T(8,128)(2,1)} %add_convert_fusion.2), channel_id=1, source_target_pairs={{0,4},{4,8},{8,12},{12,0},{1,5},{5,9},{9,13},{13,1},{2,6},{6,10},{... | collective-permute-start | bytes 1474568 | tf_op jit(solution)/shard_map/ppermute | solution.py:334
  132.5 7.1 %collective-permute-start.37 = (bf16[192,1536]{1,0:T(8,128)(2,1)}, bf16[192,1536]{1,0:T(8,128)(2,1)}, u32[]{:S(2)}, u32[]{:S(2)}) collective-permute-start(bf16[192,1536]{1,0:T(8,128)(2,1)} %get-tuple-element.121), channel_id=1, source_target_pairs={{0,1},{1,0},{2,3},{3,2},{4,5},{5,4},{6,7},{7,6},{8,9},{9,8},{10,11... | collective-permute-start | bytes 1769480 | tf_op jit(solution)/shard_map/ppermute | solution.py:340
  132.8 84.9 %collective-permute-start.36 = (bf16[256,768]{1,0:T(8,128)(2,1)}, bf16[256,768]{1,0:T(8,128)(2,1)}, u32[]{:S(2)}, u32[]{:S(2)}) collective-permute-start(bf16[256,768]{1,0:T(8,128)(2,1)} %add_convert_fusion.7), channel_id=1, source_target_pairs={{0,2},{1,3},{2,0},{3,1},{4,6},{5,7},{6,4},{7,5},{8,10},{9,11},{10,... | collective-permute-start | bytes 1179656 | tf_op jit(solution)/shard_map/ppermute | solution.py:337
  139.1 79.8 %collective-permute-start.39 = (bf16[256,768]{1,0:T(8,128)(2,1)}, bf16[256,768]{1,0:T(8,128)(2,1)}, u32[]{:S(2)}, u32[]{:S(2)}) collective-permute-start(bf16[256,768]{1,0:T(8,128)(2,1)} %add_convert_fusion.5), channel_id=1, source_target_pairs={{0,2},{1,3},{2,0},{3,1},{4,6},{5,7},{6,4},{7,5},{8,10},{9,11},{10,... | collective-permute-start | bytes 1179656 | tf_op jit(solution)/shard_map/ppermute | solution.py:337
  141.4 77.6 %collective-permute-start.40 = (bf16[192,768]{1,0:T(8,128)(2,1)}, bf16[192,768]{1,0:T(8,128)(2,1)}, u32[]{:S(2)}, u32[]{:S(2)}) collective-permute-start(bf16[192,768]{1,0:T(8,128)(2,1)} %add_convert_fusion.9), channel_id=1, source_target_pairs={{0,2},{1,3},{2,0},{3,1},{4,6},{5,7},{6,4},{7,5},{8,10},{9,11},{10,... | collective-permute-start | bytes 884744 | tf_op jit(solution)/shard_map/ppermute | solution.py:337
  143.8 31.4 %copy-start.28 = (bf16[3072,256]{1,0:T(8,128)(2,1)S(1)}, bf16[3072,256]{1,0:T(8,128)(2,1)}, u32[]{:S(2)}) copy-start(bf16[3072,256]{1,0:T(8,128)(2,1)} %get-tuple-element.33.refs_9_) | copy-start | bytes 4718596 | tf_op jit(solution)/shard_map/cond
  144.9 20.6 %collective-permute-start = (bf16[192,768]{1,0:T(8,128)(2,1)S(1)}, bf16[192,768]{1,0:T(8,128)(2,1)S(1)}, u32[]{:S(2)}, u32[]{:S(2)}) collective-permute-start(bf16[192,768]{1,0:T(8,128)(2,1)S(1)} %slice.108.refs_2_), channel_id=1, source_target_pairs={{0,2},{1,3},{2,0},{3,1},{4,6},{5,7},{6,4},{7,5},{8,10},{9,11},{10,... | collective-permute-start | bytes 884744 | tf_op jit(solution)/shard_map/cond/branch_1_fun/ppermute | solution.py:337
  145.5 29.6 %copy-start.26 = (bf16[3072,256]{1,0:T(8,128)(2,1)S(1)}, bf16[3072,256]{1,0:T(8,128)(2,1)}, u32[]{:S(2)}) copy-start(bf16[3072,256]{1,0:T(8,128)(2,1)} %get-tuple-element.32.refs_8_) | copy-start | bytes 4718596 | tf_op jit(solution)/shard_map/cond
  145.5 29.7 %copy-start.33 = (bf16[128,512]{1,0:T(8,128)(2,1)S(1)}, bf16[128,512]{1,0:T(8,128)(2,1)}, u32[]{:S(2)}) copy-start(bf16[128,512]{1,0:T(8,128)(2,1)} %get-tuple-element.29.refs_5_) | copy-start | bytes 393220 | tf_op jit(solution)/shard_map/cond
  146.6 19.0 %collective-permute-start.5 = (bf16[192,768]{1,0:T(8,128)(2,1)S(1)}, bf16[192,768]{1,0:T(8,128)(2,1)S(1)}, u32[]{:S(2)}, u32[]{:S(2)}) collective-permute-start(bf16[192,768]{1,0:T(8,128)(2,1)S(1)} %slice.111), channel_id=1, source_target_pairs={{0,8},{4,12},{8,0},{12,4},{1,9},{5,13},{9,1},{13,5},{2,10},{6,14},... | collective-permute-start | bytes 884744 | tf_op jit(solution)/shard_map/cond/branch_1_fun/ppermute | solution.py:334
  165.5 9.6 %collective-permute-start.1 = (bf16[192,1536]{1,0:T(8,128)(2,1)S(1)}, bf16[192,1536]{1,0:T(8,128)(2,1)S(1)}, u32[]{:S(2)}, u32[]{:S(2)}) collective-permute-start(bf16[192,1536]{1,0:T(8,128)(2,1)S(1)} %pad_maximum_fusion), channel_id=1, source_target_pairs={{0,1},{1,0},{2,3},{3,2},{4,5},{5,4},{6,7},{7,6},{8,9},{9,8},{10,11... | collective-permute-start | bytes 1769480 | tf_op jit(solution)/shard_map/cond/branch_1_fun/ppermute | solution.py:340
  165.6 9.4 %collective-permute-start.6 = (bf16[192,768]{1,0:T(8,128)(2,1)S(1)}, bf16[192,768]{1,0:T(8,128)(2,1)S(1)}, u32[]{:S(2)}, u32[]{:S(2)}) collective-permute-start(bf16[192,768]{1,0:T(8,128)(2,1)S(1)} %collective-permute-done.5.refs_2_), channel_id=1, source_target_pairs={{0,2},{1,3},{2,0},{3,1},{4,6},{5,7},{6,4},{7,5},{8,10},{9,11},{10,... | collective-permute-start | bytes 884744 | tf_op jit(solution)/shard_map/cond/branch_1_fun/ppermute | solution.py:337
  175.0 13.8 %slice-start.2 = ((s8[6291456]{0:T(1024)(128)(4,1)}), s8[4194304]{0:T(1024)(128)(4,1)S(1)}, s32[]{:S(2)}) async-start(s8[6291456]{0:T(1024)(128)(4,1)} %bitcast.71), calls=%async_computation.2 | async-start | bytes 8388608 | tf_op jit(solution)/shard_map/cond
  175.0 13.8 %slice-start.6 = ((s8[6291456]{0:T(1024)(128)(4,1)}), s8[4194304]{0:T(1024)(128)(4,1)S(1)}, s32[]{:S(2)}) async-start(s8[6291456]{0:T(1024)(128)(4,1)} %bitcast.75), calls=%async_computation.6 | async-start | bytes 8388608 | tf_op jit(solution)/shard_map/cond
  175.0 13.7 %collective-permute-start.7 = (bf16[192,1536]{1,0:T(8,128)(2,1)S(1)}, bf16[192,1536]{1,0:T(8,128)(2,1)S(1)}, u32[]{:S(2)}, u32[]{:S(2)}) collective-permute-start(bf16[192,1536]{1,0:T(8,128)(2,1)S(1)} %pad_maximum_fusion.1), channel_id=1, source_target_pairs={{0,1},{1,0},{2,3},{3,2},{4,5},{5,4},{6,7},{7,6},{8,9},{9,8},{10,11... | collective-permute-start | bytes 1769480 | tf_op jit(solution)/shard_map/cond/branch_1_fun/ppermute | solution.py:340
  175.1 13.6 %slice-start.3 = ((s8[6291456]{0:T(1024)(128)(4,1)}), s8[2097152]{0:T(1024)(128)(4,1)S(1)}, s32[]{:S(2)}) async-start(s8[6291456]{0:T(1024)(128)(4,1)} %bitcast.71), calls=%async_computation.3 | async-start | bytes 4194304 | tf_op jit(solution)/shard_map/cond
  175.2 13.6 %slice-start.7 = ((s8[6291456]{0:T(1024)(128)(4,1)}), s8[2097152]{0:T(1024)(128)(4,1)S(1)}, s32[]{:S(2)}) async-start(s8[6291456]{0:T(1024)(128)(4,1)} %bitcast.75), calls=%async_computation.7 | async-start | bytes 4194304 | tf_op jit(solution)/shard_map/cond
  175.2 13.6 %copy-start.34 = (bf16[128,512]{1,0:T(8,128)(2,1)S(1)}, bf16[128,512]{1,0:T(8,128)(2,1)}, u32[]{:S(2)}) copy-start(bf16[128,512]{1,0:T(8,128)(2,1)} %get-tuple-element.39.refs_5_) | copy-start | bytes 393220 | tf_op jit(solution)/shard_map/cond
  187.9 9.4 %collective-permute-start.2 = (bf16[192,1536]{1,0:T(8,128)(2,1)S(1)}, bf16[192,1536]{1,0:T(8,128)(2,1)S(1)}, u32[]{:S(2)}, u32[]{:S(2)}) collective-permute-start(bf16[192,1536]{1,0:T(8,128)(2,1)S(1)} %get-tuple-element.36), channel_id=1, source_target_pairs={{0,1},{1,0},{2,3},{3,2},{4,5},{5,4},{6,7},{7,6},{8,9},{9,8},{10,11... | collective-permute-start | bytes 1769480 | tf_op jit(solution)/shard_map/cond/branch_1_fun/ppermute | solution.py:340
  197.3 2.0 collective-permute-start.8
  197.5 9.9 %collective-permute-start.3 = (bf16[192,768]{1,0:T(8,128)(2,1)S(1)}, bf16[192,768]{1,0:T(8,128)(2,1)S(1)}, u32[]{:S(2)}, u32[]{:S(2)}) collective-permute-start(bf16[192,768]{1,0:T(8,128)(2,1)S(1)} %slice.249), channel_id=1, source_target_pairs={{0,2},{1,3},{2,0},{3,1},{4,6},{5,7},{6,4},{7,5},{8,10},{9,11},{10,... | collective-permute-start | bytes 884744 | tf_op jit(solution)/shard_map/cond/branch_1_fun/ppermute | solution.py:337
  199.5 13.8 %collective-permute-start.9 = (bf16[192,768]{1,0:T(8,128)(2,1)S(1)}, bf16[192,768]{1,0:T(8,128)(2,1)S(1)}, u32[]{:S(2)}, u32[]{:S(2)}) collective-permute-start(bf16[192,768]{1,0:T(8,128)(2,1)S(1)} %slice.248), channel_id=1, source_target_pairs={{0,2},{1,3},{2,0},{3,1},{4,6},{5,7},{6,4},{7,5},{8,10},{9,11},{10,... | collective-permute-start | bytes 884744 | tf_op jit(solution)/shard_map/cond/branch_1_fun/ppermute | solution.py:337
  207.5 10.2 %collective-permute-start.4 = (bf16[192,768]{1,0:T(8,128)(2,1)S(1)}, bf16[192,768]{1,0:T(8,128)(2,1)}, u32[]{:S(2)}, u32[]{:S(2)}) collective-permute-start(bf16[192,768]{1,0:T(8,128)(2,1)S(1)} %fusion.1), channel_id=1, source_target_pairs={{0,4},{4,8},{8,12},{12,0},{1,5},{5,9},{9,13},{13,1},{2,6},{6,10},{... | collective-permute-start | bytes 884744 | tf_op jit(solution)/shard_map/cond/branch_1_fun/ppermute | solution.py:334
  217.7 15.7 %collective-permute-start.35 = (bf16[384,768]{1,0:T(8,128)(2,1)}, bf16[384,768]{1,0:T(8,128)(2,1)S(1)}, u32[]{:S(2)}, u32[]{:S(2)}) collective-permute-start(bf16[384,768]{1,0:T(8,128)(2,1)} %add_convert_fusion), channel_id=1, source_target_pairs={{0,4},{4,8},{8,12},{12,0},{1,5},{5,9},{9,13},{13,1},{2,6},{6,10},{... | collective-permute-start | bytes 1769480 | tf_op jit(solution)/shard_map/ppermute | solution.py:334
  (20 other events, 119.1 us)
